TPU v7x, 512 devices: a whole 4x8x8 slice. The times are simulated.
512 devices in a mesh: az: 128 (over z, x, y_hi), ch: 4 (over y_lo, core).
Axes of the slice: x: 4, y: 8 (y_hi: 4, y_lo: 2; y = y_hi * 2 + y_lo), z: 8, core: 2. Of those that a mesh axis runs over, the one named last changes fastest.
Arguments:
- features: bfloat16 [256, 512, 256], P(None, 'az'), may hold values from -6 to 6
- conv1_weight: bfloat16 [256, 3, 3, 256], P('ch'), may hold values from -0.125 to 0.125
- conv1_bias: float32 [256], P('ch'), may hold values from -3 to 3
- conv2_weight: bfloat16 [256, 3, 3, 256], P('ch'), may hold values from -0.125 to 0.125
- conv2_bias: float32 [256], P('ch'), may hold values from -3 to 3
- request_cell: int32 [524288], P('az'), may hold values from 0 to 1023, as said below
- corner_slot: int32 [4, 65536], P(None, 'az'), may hold values from 0 to 4095, as said below
- corner_frac: float32 [2, 65536], P(None, 'az'), may hold values from 0 to 1
- expand_weight: bfloat16 [256, 512], P('ch'), may hold values from -0.375 to 0.375
- expand_bias: float32 [512], P('ch'), may hold values from -3 to 3
Outputs:
- occupancy: bfloat16 [512, 65536], P('ch', 'az')
Inputs may be any that keep to these rules, and one draw needn't show every extreme that they name: `request_cell`: cell index a * 256 + r within the sector that the slot's block names; entries of slots that no corner_slot entry names are never read. `corner_slot`: within one tile the 2048 entries name distinct slots; at most 32 slots of one sector block are named, exactly 32 for some sector of every tile.
All inputs are finite; a program needn't handle non-finite values.
Results may differ from a plain program's by a relative error of at most 0.014.
Values may be sent and summed in bfloat16 or wider, within the bound.
A program may use at most 64 MiB of HBM per device.

v0:
```python
import jax
import jax.numpy as jnp
from jax import lax
from jax.sharding import PartitionSpec as P


def padded_2(array, sides, width):
    for axis, dim in sides:
        size, length = (lax.axis_size(axis), array.shape[dim])
        up = [(i, (i + 1) % size) for i in range(size)]
        down = [(j, i) for i, j in up]
        last = lax.slice_in_dim(array, length - width, length, axis=dim)
        first = lax.slice_in_dim(array, 0, width, axis=dim)
        before = lax.ppermute(last, axis, up)
        after = lax.ppermute(first, axis, down)
        array = jnp.concatenate([before, array, after], axis=dim)
    return array


def convolve(padded, weight, columns, ranges):
    inputs = padded.shape[0]
    ranged = jnp.pad(padded, ((0, 0), (0, 0), (1, 1)))
    running = jnp.zeros((weight.shape[0], columns * ranges), jnp.float32)
    for tap_az in range(3):
        for tap_rg in range(3):
            window = ranged[:, tap_az : tap_az + columns, tap_rg : tap_rg + ranges].reshape(
                inputs, columns * ranges
            )
            running = running + jnp.dot(
                weight[:, tap_az, tap_rg, :], window, preferred_element_type=jnp.float32
            )
    return running


def local(
    features,
    conv1_weight,
    conv1_bias,
    conv2_weight,
    conv2_bias,
    request_cell,
    corner_slot,
    corner_frac,
    expand_weight,
    expand_bias,
):
    columns = features.shape[1]
    ranges = features.shape[2]
    outputs = conv1_weight.shape[0]
    widened = padded_2(features, (("az", 1),), 1)
    hidden_one = jax.nn.relu(
        convolve(widened, conv1_weight, columns, ranges) + conv1_bias[:, None]
    ).astype(jnp.bfloat16)
    hidden_one = padded_2(hidden_one.reshape(outputs, columns, ranges), (("az", 1),), 1)
    second_sum = convolve(
        lax.all_gather(hidden_one, "ch", axis=0, tiled=True), conv2_weight, columns, ranges
    )
    hidden_two = jax.nn.relu(second_sum + conv2_bias[:, None]).astype(jnp.bfloat16)
    asked_cells = lax.all_to_all(request_cell, "az", split_axis=0, concat_axis=0, tiled=True)
    picked_cells = jnp.take(hidden_two, asked_cells, axis=1)
    arrived = lax.all_to_all(picked_cells, "az", split_axis=1, concat_axis=1, tiled=True)
    frac_range = corner_frac[0][None, :]
    frac_azim = corner_frac[1][None, :]
    weights = [
        (1.0 - frac_range) * (1.0 - frac_azim),
        frac_range * (1.0 - frac_azim),
        (1.0 - frac_range) * frac_azim,
        frac_range * frac_azim,
    ]
    resampled = jnp.zeros((outputs, corner_slot.shape[1]), jnp.float32)
    for k in range(4):
        resampled = resampled + weights[k] * jnp.take(arrived, corner_slot[k], axis=1).astype(
            jnp.float32
        )
    resampled = resampled.astype(jnp.bfloat16)
    share_rows = expand_weight.shape[1] // lax.axis_size("ch")
    partial_term = lax.dot_general(
        expand_weight, resampled, (((0,), (0,)), ((), ())), preferred_element_type=jnp.float32
    )
    summed = lax.psum(partial_term.astype(jnp.bfloat16), "ch").astype(jnp.float32)
    own_rows = lax.dynamic_slice_in_dim(summed, lax.axis_index("ch") * share_rows, share_rows, 0)
    return (own_rows + expand_bias[:, None]).astype(jnp.bfloat16)


def solution(mesh):
    return jax.shard_map(
        local,
        mesh=mesh,
        in_specs=(
            P(None, "az", None),
            P("ch", None, None, None),
            P("ch"),
            P("ch", None, None, None),
            P("ch"),
            P("az"),
            P(None, "az"),
            P(None, "az"),
            P("ch", None),
            P("ch"),
        ),
        out_specs=P("ch", "az"),
        check_vma=False,
    )
```

profile of v0, /device:TPU:1, one launch (start us, length us, event | category | flops | bytes accessed | tf_op | source)
XLA Modules:
  0.0 193.8 jit_solution(11583841178571506555)
XLA Ops:
  6.5 1.7 fusion.78
  8.3 5.0 %collective-permute-start = (bf16[256,1,256]{2,1,0:T(2,128)(2,1)S(1)}, bf16[256,1,256]{2,1,0:T(2,128)(2,1)S(1)}, u32[]{:S(2)}, u32[]{:S(2)}) collective-permute-start(bf16[256,1,256]{2,1,0:T(2,128)(2,1)S(1)} %get-tuple-element.23), channel_id=1, source_target_pairs={{0,4},{4,8},{8,12},{12,16},{16,20},{20,24},{24,28},{28,32},{32,36}... | collective-permute-start | bytes 393224 | tf_op jit(solution)/shard_map/ppermute | solution.py:14
  13.3 14.3 %collective-permute-start.1 = (bf16[256,1,256]{2,1,0:T(2,128)(2,1)S(1)}, bf16[256,1,256]{2,1,0:T(2,128)(2,1)S(1)}, u32[]{:S(2)}, u32[]{:S(2)}) collective-permute-start(bf16[256,1,256]{2,1,0:T(2,128)(2,1)S(1)} %get-tuple-element.24), channel_id=1, source_target_pairs={{4,0},{8,4},{12,8},{16,12},{20,16},{24,20},{28,24},{32,28},{36,32}... | collective-permute-start | bytes 393224 | tf_op jit(solution)/shard_map/ppermute | solution.py:15
  27.6 1.4 all_to_all.16
  29.0 8.9 %all-to-all-start = ((s32[128,32,1]{1,2,0:T(1,128)}), s32[128,32,1]{1,2,0:T(1,128)S(1)}, u32[]{:S(2)}, u32[]{:S(2)}) async-start(s32[128,32,1]{1,2,0:T(1,128)} %bitcast.2), calls=%async_computation | async-start | bytes 131072 | tf_op jit(solution)/shard_map/all_to_all | solution.py:59
  38.4 12.6 %all-to-all-done = s32[128,32,1]{1,2,0:T(1,128)S(1)} async-done(((s32[128,32,1]{1,2,0:T(1,128)}), s32[128,32,1]{1,2,0:T(1,128)S(1)}, u32[]{:S(2)}, u32[]{:S(2)}) %all-to-all-start) | async-done | bytes 16416 | tf_op jit(solution)/shard_map/all_to_all | solution.py:59
  51.0 0.5 broadcast.128
  51.5 0.8 reduce.3
  52.5 2.4 %fusion.5 = bf16[256,6,258]{2,1,0:T(8,128)(2,1)S(1)} fusion(bf16[256,1,256]{2,1,0:T(2,128)(2,1)S(1)} %collective-permute-done.1, bf16[256,4,256]{2,1,0:T(4,128)(2,1)S(1)} %copy-done.1, bf16[256,1,256]{2,1,0:T(2,128)(2,1)S(1)} %collective-permute-done), kind=kLoop, calls=%fused_computation.12 | loop fusion | flops 4755456 | bytes 1579008 | tf_op jit(solution)/shard_map/concatenate | solution.py:16
  54.9 1.8 fusion.77
  57.1 1.2 pad_maximum_fusion
  58.9 0.2 convolution_add_fusion.2
  59.1 0.2 convolution_add_fusion.1
  59.4 0.2 fusion.13
  59.6 0.2 fusion.11
  59.8 0.2 fusion.10
  60.0 0.2 fusion.9
  60.3 0.2 fusion.17
  60.5 2.2 %collective-permute-start.2 = (bf16[64,1,256]{2,0,1:T(8,128)(2,1)S(1)}, bf16[64,1,256]{2,0,1:T(8,128)(2,1)S(1)}, u32[]{:S(2)}, u32[]{:S(2)}) collective-permute-start(bf16[64,1,256]{2,0,1:T(8,128)(2,1)S(1)} %get-tuple-element.25), channel_id=1, source_target_pairs={{0,4},{4,8},{8,12},{12,16},{16,20},{20,24},{24,28},{28,32},{32,36}... | collective-permute-start | bytes 98312 | tf_op jit(solution)/shard_map/ppermute | solution.py:14
  62.7 9.4 %collective-permute-start.3 = (bf16[64,1,256]{2,0,1:T(8,128)(2,1)S(1)}, bf16[64,1,256]{2,0,1:T(8,128)(2,1)S(1)}, u32[]{:S(2)}, u32[]{:S(2)}) collective-permute-start(bf16[64,1,256]{2,0,1:T(8,128)(2,1)S(1)} %get-tuple-element.26), channel_id=1, source_target_pairs={{4,0},{8,4},{12,8},{16,12},{20,16},{24,20},{28,24},{32,28},{36,32}... | collective-permute-start | bytes 98312 | tf_op jit(solution)/shard_map/ppermute | solution.py:15
  72.2 1.0 collective-permute-done.3
  73.2 11.6 %all_gather.3 = bf16[256,6,256]{2,0,1:T(8,128)(2,1)S(1)} all-gather(bf16[64,6,256]{2,0,1:T(8,128)(2,1)S(1)} %pad_maximum_fusion.2), channel_id=1, replica_groups=mesh['az'=128,'ch'=4] {'ch'}, dimensions={0}, use_global_device_ids=true | all-gather | bytes 983040 | tf_op jit(solution)/shard_map/all_gather | solution.py:56
  84.8 0.3 copy.25
  85.1 0.6 pad_slice_fusion
  85.7 0.3 copy-done.2
  86.0 0.3 fusion.45
  86.3 0.3 convolution_add_fusion.10
  86.6 0.3 convolution_add_fusion.9
  86.9 0.3 convolution_add_fusion.8
  87.1 0.3 convolution_add_fusion.7
  87.4 0.3 convolution_add_fusion.6
  87.7 0.3 convolution_add_fusion.5
  88.0 0.3 convolution_add_fusion.4
  88.3 0.3 fusion.19
  88.8 12.1 %gather_fusion = bf16[4096,64]{1,0:T(8,128)(2,1)S(1)} fusion(bf16[64,1024]{0,1:T(8,128)(2,1)S(1)} %copy.29, s32[4096]{0:T(1024)S(1)} %broadcast_clamp_fusion), kind=kCustom, calls=%fused_computation.4 | custom fusion | bytes 1064960 | tf_op jit(solution)/shard_map/jit(_take)/gather | solution.py:60
  100.9 0.8 fusion.81
  101.8 1.4 reshape.189
  103.1 12.0 %all-to-all-start.1 = ((bf16[128,2,1024]{2,1,0:T(2,128)(2,1)}), bf16[128,2,1024]{2,1,0:T(2,128)(2,1)S(1)}, u32[]{:S(2)}, u32[]{:S(2)}) async-start(bf16[128,2,1024]{2,1,0:T(2,128)(2,1)} %reshape.189), calls=%async_computation.1 | async-start | bytes 1048576 | tf_op jit(solution)/shard_map/all_to_all | solution.py:61
  115.3 19.0 %all-to-all-done.1 = bf16[128,2,1024]{2,1,0:T(2,128)(2,1)S(1)} async-done(((bf16[128,2,1024]{2,1,0:T(2,128)(2,1)}), bf16[128,2,1024]{2,1,0:T(2,128)(2,1)S(1)}, u32[]{:S(2)}, u32[]{:S(2)}) %all-to-all-start.1) | async-done | bytes 524320 | tf_op jit(solution)/shard_map/all_to_all | solution.py:61
  134.3 0.6 reshape.190
  134.9 1.3 gather_fusion.1
  136.2 1.3 gather_fusion.2
  137.6 1.3 gather_fusion.3
  138.9 1.3 gather_fusion.4
  140.3 1.7 fusion.6
  142.0 43.2 %all-reduce.4.cloned.1.call-done = bf16[512,512]{0,1:T(8,128)(2,1)} async-done(((bf16[512,512]{0,1:T(8,128)(2,1)}), bf16[512,512]{0,1:T(8,128)(2,1)}) %all-reduce.4.cloned.1.call-update) | async-done | bytes 524304 | tf_op jit(solution)/shard_map/psum | solution.py:80
  185.3 0.9 add_convert_fusion
  186.2 0.8 copy.30
  (53 shorter events, 1.8 us)
Async XLA Ops:
  6.5 133.8 %copy-start = (bf16[64,512]{1,0:T(8,128)(2,1)S(1)}, bf16[64,512]{1,0:T(8,128)(2,1)}, u32[]{:S(2)}) copy-start(bf16[64,512]{1,0:T(8,128)(2,1)} %param.20) | copy-start | bytes 196612
  6.5 31.4 %copy-start.1 = (bf16[256,4,256]{2,1,0:T(4,128)(2,1)S(1)}, bf16[256,4,256]{2,1,0:T(4,128)(2,1)}, u32[]{:S(2)}) copy-start(bf16[256,4,256]{2,1,0:T(4,128)(2,1)} %param.12) | copy-start | bytes 1572868
  6.5 31.5 %copy-start.4 = (s32[4,512]{1,0:T(4,128)S(1)}, s32[4,512]{1,0:T(4,128)}, u32[]{:S(2)}) copy-start(s32[4,512]{1,0:T(4,128)} %param.18) | copy-start | bytes 24580
  6.5 31.6 %copy-start.3 = (bf16[64,3,3,256]{3,0,2,1:T(8,128)(2,1)S(1)}, bf16[64,3,3,256]{3,0,2,1:T(8,128)(2,1)}, u32[]{:S(2)}) copy-start(bf16[64,3,3,256]{3,0,2,1:T(8,128)(2,1)} %param.13) | copy-start | bytes 884740
  8.3 44.2 %collective-permute-start = (bf16[256,1,256]{2,1,0:T(2,128)(2,1)S(1)}, bf16[256,1,256]{2,1,0:T(2,128)(2,1)S(1)}, u32[]{:S(2)}, u32[]{:S(2)}) collective-permute-start(bf16[256,1,256]{2,1,0:T(2,128)(2,1)S(1)} %get-tuple-element.23), channel_id=1, source_target_pairs={{0,4},{4,8},{8,12},{12,16},{16,20},{20,24},{24,28},{28,32},{32,36}... | collective-permute-start | bytes 393224 | tf_op jit(solution)/shard_map/ppermute | solution.py:14
  13.3 39.2 %collective-permute-start.1 = (bf16[256,1,256]{2,1,0:T(2,128)(2,1)S(1)}, bf16[256,1,256]{2,1,0:T(2,128)(2,1)S(1)}, u32[]{:S(2)}, u32[]{:S(2)}) collective-permute-start(bf16[256,1,256]{2,1,0:T(2,128)(2,1)S(1)} %get-tuple-element.24), channel_id=1, source_target_pairs={{4,0},{8,4},{12,8},{16,12},{20,16},{24,20},{28,24},{32,28},{36,32}... | collective-permute-start | bytes 393224 | tf_op jit(solution)/shard_map/ppermute | solution.py:15
  29.0 22.0 %all-to-all-start = ((s32[128,32,1]{1,2,0:T(1,128)}), s32[128,32,1]{1,2,0:T(1,128)S(1)}, u32[]{:S(2)}, u32[]{:S(2)}) async-start(s32[128,32,1]{1,2,0:T(1,128)} %bitcast.2), calls=%async_computation | async-start | bytes 131072 | tf_op jit(solution)/shard_map/all_to_all | solution.py:59
  59.6 0.7 copy-start.6
  60.5 11.6 %collective-permute-start.2 = (bf16[64,1,256]{2,0,1:T(8,128)(2,1)S(1)}, bf16[64,1,256]{2,0,1:T(8,128)(2,1)S(1)}, u32[]{:S(2)}, u32[]{:S(2)}) collective-permute-start(bf16[64,1,256]{2,0,1:T(8,128)(2,1)S(1)} %get-tuple-element.25), channel_id=1, source_target_pairs={{0,4},{4,8},{8,12},{12,16},{16,20},{20,24},{24,28},{28,32},{32,36}... | collective-permute-start | bytes 98312 | tf_op jit(solution)/shard_map/ppermute | solution.py:14
  62.7 10.4 %collective-permute-start.3 = (bf16[64,1,256]{2,0,1:T(8,128)(2,1)S(1)}, bf16[64,1,256]{2,0,1:T(8,128)(2,1)S(1)}, u32[]{:S(2)}, u32[]{:S(2)}) collective-permute-start(bf16[64,1,256]{2,0,1:T(8,128)(2,1)S(1)} %get-tuple-element.26), channel_id=1, source_target_pairs={{4,0},{8,4},{12,8},{16,12},{20,16},{24,20},{28,24},{32,28},{36,32}... | collective-permute-start | bytes 98312 | tf_op jit(solution)/shard_map/ppermute | solution.py:15
  85.0 1.0 copy-start.2
  87.4 0.9 copy-start.7
  101.7 13.5 %copy-start.5 = (f32[2,512]{1,0:T(2,128)S(1)}, f32[2,512]{1,0:T(2,128)}, u32[]{:S(2)}) copy-start(f32[2,512]{1,0:T(2,128)} %param.19) | copy-start | bytes 12292
  103.1 31.1 %all-to-all-start.1 = ((bf16[128,2,1024]{2,1,0:T(2,128)(2,1)}), bf16[128,2,1024]{2,1,0:T(2,128)(2,1)S(1)}, u32[]{:S(2)}, u32[]{:S(2)}) async-start(bf16[128,2,1024]{2,1,0:T(2,128)(2,1)} %reshape.189), calls=%async_computation.1 | async-start | bytes 1048576 | tf_op jit(solution)/shard_map/all_to_all | solution.py:61
  115.1 70.1 %all-reduce.4.cloned.1.call-start = ((), (), s32[]{:S(2)}) async-start(), calls=%async_computation.2 | async-start | bytes 1048576 | tf_op jit(solution)/shard_map/psum | solution.py:80
  137.6 47.7 %copy-start.8 = (f32[128]{0:T(128)S(1)}, f32[128]{0:T(128)}, u32[]{:S(2)}) copy-start(f32[128]{0:T(128)} %param.21) | copy-start | bytes 1540
Sparse Core Ops, SparseCore 0:
  142.1 43.0 all-reduce.3
where the time goes:
time: 194 us
  waiting for transfers between devices  75.9 us (39%)
  starting transfers between devices  51.8 us (27%)
  local copies, waits for them, and re-layouts  28.1 us (14%)
  between operations  14 us (7%)
  blocking collectives  11.6 us (6%)
  other arithmetic  6.25 us (3%)
  matrix products  6.14 us (3%)
    psum x1, waiting for transfers between devices, local(): lax.psum(partial_term.astype(jnp.bfloat16), 'ch').astype(jnp.float32)  43.2 us
    ppermute x2, starting transfers between devices, padded_2(): after = lax.ppermute(first, axis, down)  23.7 us
    all_to_all x1, waiting for transfers between devices, local(): lax.all_to_all(picked_cells, 'az', split_axis=1, concat_axis=1, tiled=True)  19 us
    all_to_all x1, waiting for transfers between devices, local(): lax.all_to_all(request_cell, 'az', split_axis=0, concat_axis=0, tiled=True)  12.6 us
    gather x1, local copies, waits for them, and re-layouts, local(): picked_cells = jnp.take(hidden_two, asked_cells, axis=1)  12.1 us
    all_to_all x1, starting transfers between devices, local(): lax.all_to_all(picked_cells, 'az', split_axis=1, concat_axis=1, tiled=True)  12 us
    all_gather x1, blocking collectives, local(): lax.all_gather(hidden_one, 'ch', axis=0, tiled=True)  11.6 us
    all_to_all x1, starting transfers between devices, local(): lax.all_to_all(request_cell, 'az', split_axis=0, concat_axis=0, tiled=True)  8.91 us
  transfers between devices with their start and end apart: 7, of which 4 were waited for; matrix products, arithmetic and copies ran while one was open for 1% of the time, Pallas kernels for 0%

commit v1 on v0

v1 whole, which is shorter than its diff:
```python
import functools

import jax
import jax.numpy as jnp
from jax import lax
from jax.experimental import pallas as pl
from jax.experimental.pallas import tpu as pltpu
from jax.sharding import PartitionSpec as P

MESH = pl.DeviceIdType.MESH
BF = jnp.bfloat16
F32 = jnp.float32
HALF = 16


def group_of(n):
    return 8 if n % 64 == 0 else 2


def combine(acc, rows, ranges):
    lane = lax.broadcasted_iota(jnp.int32, (rows, ranges), 1)
    low = jnp.where(lane == 0, 0.0, pltpu.roll(acc[:rows], 1, 1))
    high = jnp.where(lane == ranges - 1, 0.0, pltpu.roll(acc[2 * rows :], ranges - 1, 1))
    return low + acc[rows : 2 * rows] + high


def column_of(row):
    k = row.shape[1]
    a = lax.broadcasted_iota(jnp.int32, (k, k), 0)
    b = lax.broadcasted_iota(jnp.int32, (k, k), 1)
    return jnp.sum(jnp.where(a == b, jnp.broadcast_to(row, (k, k)), 0.0), axis=1, keepdims=True)


def kernel(
    n,
    feat,
    w1,
    b1,
    w2,
    b2,
    req,
    slot,
    frac,
    wexp,
    bexp,
    out,
    h1,
    e1s,
    e1r,
    e2s,
    e2r,
    acc_edge,
    oha,
    ohb,
    sa,
    sb,
    keyt,
    wt,
    reqt,
    pbuf,
    arr,
    h2t,
    rq,
    wr,
    wx,
    rbuf,
    e1_send,
    e1_recv,
    e2_send,
    e2_recv,
    rq_send,
    rq_recv,
    w_send,
    w_recv,
    g_send,
    g_recv,
    r_send,
    r_recv,
    a_send,
    a_recv,
):
    az = lax.axis_index("az")
    ch = lax.axis_index("ch")
    chans = feat.shape[0] // 4
    ranges = feat.shape[1]
    outs = w1.shape[0] // 3
    cart = slot.shape[1]
    groups = group_of(n)
    members = n // groups
    rows = members * HALF
    hh = out.shape[0]
    right = lax.rem(az + 1, n)
    left = lax.rem(az + n - 1, n)

    barrier = pltpu.get_barrier_semaphore()

    def greet(d, _):
        pl.semaphore_signal(
            barrier, inc=1, device_id=(lax.rem(az + d, n), ch), device_id_type=MESH
        )
        return 0

    lax.fori_loop(1, n, greet, 0)
    for d in range(1, 4):
        pl.semaphore_signal(
            barrier, inc=1, device_id=(az, lax.rem(ch + d, 4)), device_id_type=MESH
        )

    def part(w, x, col):
        lo, hi = max(col - 1, 0), min(col + 1, 3)
        first = lo - (col - 1)
        return jnp.dot(
            w[:, first * chans : (first + hi - lo + 1) * chans],
            x[lo * chans : (hi + 1) * chans, :],
            preferred_element_type=F32,
        )

    e1s[0] = combine(part(w1, feat, 4), outs, ranges).astype(BF)
    e1s[1] = combine(part(w1, feat, -1), outs, ranges).astype(BF)

    pl.semaphore_wait(barrier, n + 2)

    def edge(src, dst, send, recv):
        copies = []
        for k, to in ((0, right), (1, left)):
            copies.append(
                pltpu.make_async_remote_copy(
                    src_ref=src.at[k],
                    dst_ref=dst.at[k],
                    send_sem=send.at[k],
                    recv_sem=recv.at[k],
                    device_id=(to, ch),
                    device_id_type=MESH,
                )
            )
        return copies

    e1 = edge(e1s, e1r, e1_send, e1_recv)
    for c in e1:
        c.start()

    def ask(d, _):
        to = lax.rem(az + d, n)
        pltpu.make_async_remote_copy(
            src_ref=req.at[to],
            dst_ref=rq.at[az],
            send_sem=rq_send,
            recv_sem=rq_recv,
            device_id=(to, ch),
            device_id_type=MESH,
        ).start()
        return 0

    lax.fori_loop(1, n, ask, 0)
    wcopies = []
    for d in range(1, 4):
        to = lax.rem(ch + d, 4)
        c = pltpu.make_async_remote_copy(
            src_ref=wexp.at[to],
            dst_ref=wr.at[ch],
            send_sem=w_send.at[d - 1],
            recv_sem=w_recv.at[d - 1],
            device_id=(az, to),
            device_id_type=MESH,
        )
        c.start()
        wcopies.append(c)
    wr[ch] = wexp[ch]
    rq[az] = req[az]

    bias1 = column_of(b1[...])
    bias2 = column_of(b2[...])

    def finish(total, bias):
        return jnp.maximum(total + bias, 0.0).astype(BF)

    def mine(col):
        return pl.ds(pl.multiple_of(col * chans + ch * outs, outs), outs)

    def spread(col):
        copies = []
        for d in range(1, 4):
            c = pltpu.make_async_remote_copy(
                src_ref=h1.at[mine(col)],
                dst_ref=h1.at[mine(col)],
                send_sem=g_send.at[col, d - 1],
                recv_sem=g_recv.at[col, d - 1],
                device_id=(az, lax.rem(ch + d, 4)),
                device_id_type=MESH,
            )
            c.start()
            copies.append(c)
        return copies

    gathers = {}
    for col in (1, 2):
        h1[mine(col), :] = finish(combine(part(w1, feat, col), outs, ranges), bias1)
        gathers[col] = spread(col)
    for k, col in ((0, 0), (1, 3)):
        acc_edge[k] = combine(part(w1, feat, col), outs, ranges) + bias1
    for k, col in ((0, 0), (1, 3)):
        e1[k].wait_recv()
        h1[mine(col), :] = jnp.maximum(acc_edge[k] + e1r[k].astype(F32), 0.0).astype(BF)
        gathers[col] = spread(col)

    q = slot[...]
    m = lax.shift_left(lax.shift_right_logical(q, 5), 4) + jnp.bitwise_and(q, 15)
    upper = jnp.bitwise_and(q, 16) != 0
    keys = jnp.concatenate(
        [jnp.where(upper, -1, m), jnp.where(upper, m, -1)]
        + [jnp.zeros((120, cart), jnp.int32)],
        axis=0,
    )
    keyt[...] = keys.T
    u, v = frac[0:1, :], frac[1:2, :]
    weights = jnp.concatenate(
        [(1.0 - u) * (1.0 - v), u * (1.0 - v), (1.0 - u) * v, u * v]
        + [jnp.zeros((124, cart), F32)],
        axis=0,
    )
    wt[...] = weights.T

    def s_rows(b, _):
        at = pl.ds(pl.multiple_of(b * 16, 16), 16)
        spot = lax.broadcasted_iota(jnp.int32, (16, n * HALF), 1)
        for base, ref in ((0, sa), (4, sb)):
            total = jnp.zeros((16, n * HALF), F32)
            for k in range(4):
                key = keyt[at, base + k : base + k + 1]
                total = jnp.where(spot == key, wt[at, k : k + 1], total)
            ref[at, :] = total.astype(BF)
        return 0

    lax.fori_loop(0, cart // 16, s_rows, 0)

    for d in range(3):
        wcopies[d].wait_recv()
    for g in range(4):
        block = wr[g].astype(F32)
        zero = jnp.zeros((128 - outs, hh), F32)
        wx[0, :, g * 128 : (g + 1) * 128] = jnp.concatenate([block, zero], axis=0).T.astype(BF)
        wx[1, :, g * 128 : (g + 1) * 128] = jnp.concatenate([zero, block], axis=0).T.astype(BF)
    bias3 = column_of(bexp[...])

    for col in (3, 0):
        for c in gathers[col]:
            c.wait_recv()
    e2s[0] = combine(part(w2, h1, 4), outs, ranges).astype(BF)
    e2s[1] = combine(part(w2, h1, -1), outs, ranges).astype(BF)
    e2 = edge(e2s, e2r, e2_send, e2_recv)
    for c in e2:
        c.start()
    for col in (1, 2):
        for c in gathers[col]:
            c.wait_recv()

    def place(col, value):
        zero = jnp.zeros((128 - outs, ranges), F32)
        at = slice(col * ranges, (col + 1) * ranges)
        h2t[0, at, :] = jnp.concatenate([value, zero], axis=0).T.astype(BF)
        h2t[1, at, :] = jnp.concatenate([zero, value], axis=0).T.astype(BF)

    for col in (1, 2):
        place(col, jnp.maximum(combine(part(w2, h1, col), outs, ranges) + bias2, 0.0))
    for k, col in ((0, 0), (1, 3)):
        acc_edge[k] = combine(part(w2, h1, col), outs, ranges) + bias2

    pltpu.make_async_remote_copy(
        src_ref=req.at[pl.ds(0, n - 1)],
        dst_ref=rq.at[pl.ds(0, n - 1)],
        send_sem=rq_send,
        recv_sem=rq_recv,
        device_id=(right, ch),
        device_id_type=MESH,
    ).wait_recv()
    reqt[...] = rq[:, 0, :].T

    def one_hot(t, _):
        turned = pltpu.roll(reqt[...], lax.rem(n - t, n), 1)
        spot = lax.broadcasted_iota(jnp.int32, (HALF, 4 * ranges), 1)
        at = pl.ds(pl.multiple_of(t * HALF, HALF), HALF)
        oha[at, :] = jnp.where(spot == turned[:HALF, 0:1], 1.0, 0.0).astype(BF)
        ohb[at, :] = jnp.where(spot == turned[HALF : 2 * HALF, 0:1], 1.0, 0.0).astype(BF)
        return 0

    lax.fori_loop(0, n, one_hot, 0)

    for k, col in ((0, 0), (1, 3)):
        e2[k].wait_recv()
        place(col, jnp.maximum(acc_edge[k] + e2r[k].astype(F32), 0.0))

    plane = az // members
    inner = lax.rem(az, members)
    for dz in range(groups):
        to_plane = lax.rem(plane + dz, groups)
        at = pl.ds(pl.multiple_of(to_plane * rows, rows), rows)
        picked = jnp.dot(oha[at, :], h2t[0], preferred_element_type=F32)
        picked += jnp.dot(ohb[at, :], h2t[1], preferred_element_type=F32)
        pbuf[dz] = picked.astype(BF)

        def ship(i, _):
            spot = lax.rem(inner + i, members)
            pltpu.make_async_remote_copy(
                src_ref=pbuf.at[dz, pl.ds(pl.multiple_of(spot * HALF, HALF), HALF)],
                dst_ref=arr.at[dz, pl.ds(pl.multiple_of(inner * HALF, HALF), HALF)],
                send_sem=a_send.at[dz],
                recv_sem=a_recv.at[dz],
                device_id=(to_plane * members + spot, ch),
                device_id_type=MESH,
            ).start()
            return 0

        lax.fori_loop(1 if dz == 0 else 0, members, ship, 0)
        if dz == 0:
            own = pl.ds(pl.multiple_of(inner * HALF, HALF), HALF)
            arr[0, own, :] = pbuf[0, own, :]

    def whole(dz):
        size = rows - HALF if dz == 0 else rows
        return pltpu.make_async_remote_copy(
            src_ref=pbuf.at[dz, pl.ds(0, size)],
            dst_ref=arr.at[dz, pl.ds(0, size)],
            send_sem=a_send.at[dz],
            recv_sem=a_recv.at[dz],
            device_id=(right, ch),
            device_id_type=MESH,
        )

    total_a = jnp.zeros((cart, 128), F32)
    total_b = jnp.zeros((cart, 128), F32)
    for dz in range(groups):
        whole(dz).wait_recv()
        from_plane = lax.rem(plane + groups - dz, groups)
        at = pl.ds(pl.multiple_of(from_plane * rows, rows), rows)
        total_a += jnp.dot(sa[:, at], arr[dz], preferred_element_type=F32)
        total_b += jnp.dot(sb[:, at], arr[dz], preferred_element_type=F32)

    half = cart // 2
    lane = lax.broadcasted_iota(jnp.int32, (half, 128), 1)
    first = total_a[:half] + pltpu.roll(total_b[:half], 64, 1)
    second = pltpu.roll(total_a[half:], 64, 1) + total_b[half:]
    rbuf[ch] = jnp.where(lane < 64, first, second).astype(BF)
    rcopies = []
    for d in range(1, 4):
        c = pltpu.make_async_remote_copy(
            src_ref=rbuf.at[ch],
            dst_ref=rbuf.at[ch],
            send_sem=r_send.at[d - 1],
            recv_sem=r_recv.at[d - 1],
            device_id=(az, lax.rem(ch + d, 4)),
            device_id_type=MESH,
        )
        c.start()
        rcopies.append(c)
    for c in rcopies:
        c.wait_recv()
    for p in range(2):
        sum_p = jnp.zeros((hh, half), F32)
        for g in range(4):
            sum_p += lax.dot_general(
                wx[p, :, g * 128 : (g + 1) * 128],
                rbuf[g],
                (((1,), (1,)), ((), ())),
                preferred_element_type=F32,
            )
        out[:, p * half : (p + 1) * half] = (sum_p + bias3).astype(BF)

    for c in e1 + e2 + wcopies + rcopies + [c for col in range(4) for c in gathers[col]]:
        c.wait_send()
    pltpu.make_async_remote_copy(
        src_ref=req.at[pl.ds(0, n - 1)],
        dst_ref=rq.at[pl.ds(0, n - 1)],
        send_sem=rq_send,
        recv_sem=rq_recv,
        device_id=(right, ch),
        device_id_type=MESH,
    ).wait_send()
    for dz in range(groups):
        whole(dz).wait_send()


def local(
    features,
    conv1_weight,
    conv1_bias,
    conv2_weight,
    conv2_bias,
    request_cell,
    corner_slot,
    corner_frac,
    expand_weight,
    expand_bias,
):
    n = lax.axis_size("az")
    chans, columns, ranges = features.shape
    outs = conv1_weight.shape[0]
    cart = corner_slot.shape[1]
    hh = expand_bias.shape[0]
    groups = group_of(n)
    rows = n // groups * HALF

    feat = features.transpose(1, 0, 2).reshape(columns * chans, ranges)
    w1 = conv1_weight.transpose(2, 0, 1, 3).reshape(3 * outs, 3 * chans)
    w2 = conv2_weight.transpose(2, 0, 1, 3).reshape(3 * outs, 3 * chans)
    wexp = expand_weight.reshape(outs, 4, hh).transpose(1, 0, 2)
    args = (
        feat,
        w1,
        conv1_bias.reshape(1, outs),
        w2,
        conv2_bias.reshape(1, outs),
        request_cell.reshape(n, 1, 2 * HALF),
        corner_slot,
        corner_frac,
        wexp,
        expand_bias.reshape(1, hh),
    )
    dma = pltpu.SemaphoreType.DMA
    return pl.pallas_call(
        functools.partial(kernel, n),
        out_shape=jax.ShapeDtypeStruct((hh, cart), BF),
        in_specs=[pl.BlockSpec(memory_space=pltpu.VMEM)] * len(args),
        out_specs=pl.BlockSpec(memory_space=pltpu.VMEM),
        scratch_shapes=[
            pltpu.VMEM((4 * chans, ranges), BF),
            pltpu.VMEM((2, outs, ranges), BF),
            pltpu.VMEM((2, outs, ranges), BF),
            pltpu.VMEM((2, outs, ranges), BF),
            pltpu.VMEM((2, outs, ranges), BF),
            pltpu.VMEM((2, outs, ranges), F32),
            pltpu.VMEM((n * HALF, 4 * ranges), BF),
            pltpu.VMEM((n * HALF, 4 * ranges), BF),
            pltpu.VMEM((cart, n * HALF), BF),
            pltpu.VMEM((cart, n * HALF), BF),
            pltpu.VMEM((cart, 128), jnp.int32),
            pltpu.VMEM((cart, 128), F32),
            pltpu.VMEM((2 * HALF, n), jnp.int32),
            pltpu.VMEM((groups, rows, 128), BF),
            pltpu.VMEM((groups, rows, 128), BF),
            pltpu.VMEM((2, 4 * ranges, 128), BF),
            pltpu.VMEM((n, 1, 2 * HALF), jnp.int32),
            pltpu.VMEM((4, outs, hh), BF),
            pltpu.VMEM((2, hh, 512), BF),
            pltpu.VMEM((4, cart // 2, 128), BF),
            dma((2,)),
            dma((2,)),
            dma((2,)),
            dma((2,)),
            dma,
            dma,
            dma((3,)),
            dma((3,)),
            dma((4, 3)),
            dma((4, 3)),
            dma((3,)),
            dma((3,)),
            dma((groups,)),
            dma((groups,)),
        ],
        compiler_params=pltpu.CompilerParams(
            collective_id=0, has_side_effects=True, vmem_limit_bytes=40 * 1024 * 1024
        ),
        cost_estimate=pl.CostEstimate(
            flops=4 * 10**9, bytes_accessed=2 * 10**6, transcendentals=0
        ),
    )(*args)


def solution(mesh):
    return jax.shard_map(
        local,
        mesh=mesh,
        in_specs=(
            P(None, "az", None),
            P("ch", None, None, None),
            P("ch"),
            P("ch", None, None, None),
            P("ch"),
            P("az"),
            P(None, "az"),
            P(None, "az"),
            P("ch", None),
            P("ch"),
        ),
        out_specs=P("ch", "az"),
        check_vma=False,
    )
```

time: 194 us -> 81.7 us (0.42)
  Pallas kernels: 0 us -> 75.9 us
  waiting for transfers between devices: 75.9 us -> 0 us
  starting transfers between devices: 51.8 us -> 0 us
  local copies, waits for them, and re-layouts: 28.1 us -> 5.45 us
  between operations: 14 us -> 0.07 us
  blocking collectives: 11.6 us -> 0 us
  other arithmetic: 6.25 us -> 0 us
  matrix products: 6.14 us -> 0 us
    pallas_call x0 -> x1, Pallas kernels: none -> 75.9 us  [local(): pl.pallas_call(functools.partial(kernel, n), out_shape=jax.ShapeDtypeStru...]
    psum x1 -> x0, waiting for transfers between devices: 43.2 us -> none  [local(): lax.psum(partial_term.astype(jnp.bfloat16), 'ch').astype(jnp.float32)]
    all_to_all x2 -> x0, waiting for transfers between devices: 31.6 us -> none  [the longest x1 19 us: local(): lax.all_to_all(picked_cells, 'az', split_axis=1, concat_axis=1, tiled=True)]
    ppermute x4 -> x0, starting transfers between devices: 30.9 us -> none  [the longest x2 23.7 us: padded_2(): after = lax.ppermute(first, axis, down)]
    all_to_all x2 -> x0, starting transfers between devices: 20.9 us -> none  [the longest x1 12 us: local(): lax.all_to_all(picked_cells, 'az', split_axis=1, concat_axis=1, tiled=True)]
    gather x5 -> x0, local copies, waits for them, and re-layouts: 17.5 us -> none  [the longest x1 12.1 us: local(): picked_cells = jnp.take(hidden_two, asked_cells, axis=1)]
    all_gather x1 -> x0, blocking collectives: 11.6 us -> none  [local(): lax.all_gather(hidden_one, 'ch', axis=0, tiled=True)]
    dot_general x19 -> x0, matrix products: 6.14 us -> none  [the longest x18 4.44 us: convolve(): jnp.dot(weight[:, tap_az, tap_rg, :], window, preferred_element_type=jnp....]
  transfers between devices with their start and end apart: 7 -> 0, of which waited for: 4 -> 0; matrix products, arithmetic and copies ran while one was open for 1% -> 0% of each run, Pallas kernels for 0% -> 0%
where the time goes in v1:
time: 81.7 us; the launch traced here: 81.4 us
  Pallas kernels  75.9 us (93%)
  local copies, waits for them, and re-layouts  5.45 us (7%)
    pallas_call x1, Pallas kernels, local(): pl.pallas_call(functools.partial(kernel, n), out_shape=jax.ShapeDtypeStru...  75.9 us
    unnamed x19, local copies, waits for them, and re-layouts  3.07 us

profile of v1, /device:TPU:1, one launch (start us, length us, event | category | flops | bytes accessed | tf_op | source)
XLA Modules:
  0.0 81.4 jit_solution(2159755169575782509)
XLA Ops:
  0.0 0.0 copy-start
  0.0 0.8 %reshape.29 = s32[128,1,32]{2,0,1:T(8,128)S(1)} reshape(s32[4096]{0:T(1024)} %param.15) | data formatting | bytes 32768 | tf_op jit(solution)/shard_map/reshape | solution.py:412
  0.8 0.0 copy-done
  0.9 1.2 %copy.15 = bf16[3,64,3,256]{3,2,1,0:T(4,128)(2,1)S(1)} copy(bf16[3,64,3,256]{3,1,0,2:T(8,128)(2,1)} %bitcast.31) | data formatting | bytes 589824 | tf_op jit(solution)/shard_map/transpose | solution.py:403
  2.1 0.0 copy-start.7
  2.1 0.9 %copy-done.7 = bf16[64,3,3,256]{3,0,2,1:T(8,128)(2,1)S(1)} copy-done((bf16[64,3,3,256]{3,0,2,1:T(8,128)(2,1)S(1)}, bf16[64,3,3,256]{3,0,2,1:T(8,128)(2,1)}, u32[]{:S(2)}) %copy-start.7) | copy-done | bytes 294936
  3.0 0.0 copy-start.6
  3.0 0.3 copy.16
  3.4 0.7 copy-done.6
  4.1 0.0 copy-start.1
  4.1 0.0 copy-start.2
  4.1 0.1 copy.14
  4.2 0.0 copy-start.3
  4.2 0.0 copy-start.4
  4.2 0.0 copy-start.5
  4.2 0.6 copy-done.1
  4.8 0.0 copy-done.2
  4.8 0.0 copy-done.3
  4.8 0.0 copy-done.4
  4.8 0.0 copy-done.5
  4.9 75.9 %shard_map.100 = bf16[128,512]{1,0:T(8,128)(2,1)S(1)} custom-call(bf16[1024,256]{1,0:T(8,128)(2,1)S(1)} %bitcast.21, bf16[192,768]{1,0:T(8,128)(2,1)S(1)} %bitcast.22, f32[1,64]{1,0:T(1,128)S(1)} %bitcast.25, bf16[192,768]{1,0:T(8,128)(2,1)S(1)} %bitcast.23, f32[1,64]{1,0:T(1,128)S(1)} %bitcast.26, s32[128,1,32]{2,1,0:T(1,128)S(1)} %bitcast.24, ...), custom_call_target="tpu_custom_call" | custom-call | flops 4000000000 | bytes 2000000 | tf_op jit(solution)/shard_map/pallas_call | solution.py:419
  80.8 0.7 copy.24
  (3 shorter events, 0.1 us)
Async XLA Ops:
  0.0 0.8 %copy-start = (bf16[64,512]{1,0:T(8,128)(2,1)S(1)}, bf16[64,512]{1,0:T(8,128)(2,1)}, u32[]{:S(2)}) copy-start(bf16[64,512]{1,0:T(8,128)(2,1)} %param.18) | copy-start | bytes 196612
  2.1 1.0 %copy-start.7 = (bf16[64,3,3,256]{3,0,2,1:T(8,128)(2,1)S(1)}, bf16[64,3,3,256]{3,0,2,1:T(8,128)(2,1)}, u32[]{:S(2)}) copy-start(bf16[64,3,3,256]{3,0,2,1:T(8,128)(2,1)} %param.13) | copy-start | bytes 884740
  3.0 1.0 %copy-start.6 = (bf16[256,4,256]{2,1,0:T(4,128)(2,1)S(1)}, bf16[256,4,256]{2,1,0:T(4,128)(2,1)}, u32[]{:S(2)}) copy-start(bf16[256,4,256]{2,1,0:T(4,128)(2,1)} %param.10) | copy-start | bytes 1572868
  4.1 0.7 copy-start.1
  4.1 0.7 copy-start.2
  4.2 0.7 copy-start.3
  4.2 0.7 copy-start.4
  4.2 0.7 copy-start.5

commit v2 on v1

v2 whole, which is shorter than its diff:
```python
import functools

import jax
import jax.numpy as jnp
from jax import lax
from jax.experimental import pallas as pl
from jax.experimental.pallas import tpu as pltpu
from jax.sharding import PartitionSpec as P

MESH = pl.DeviceIdType.MESH
BF = jnp.bfloat16
F32 = jnp.float32
HALF = 16


def torus(n):
    return (8, 4, 4) if n == 128 else (2, 1, n // 2)


def combine(acc, rows, ranges):
    lane = lax.broadcasted_iota(jnp.int32, (rows, ranges), 1)
    low = jnp.where(lane == 0, 0.0, pltpu.roll(acc[:rows], 1, 1))
    high = jnp.where(lane == ranges - 1, 0.0, pltpu.roll(acc[2 * rows :], ranges - 1, 1))
    return low + acc[rows : 2 * rows] + high


def column_of(row):
    k = row.shape[1]
    a = lax.broadcasted_iota(jnp.int32, (k, k), 0)
    b = lax.broadcasted_iota(jnp.int32, (k, k), 1)
    return jnp.sum(jnp.where(a == b, jnp.broadcast_to(row, (k, k)), 0.0), axis=1, keepdims=True)


def kernel(
    n,
    feat,
    w1_in,
    b1_in,
    w2_in,
    b2_in,
    req_in,
    slot_in,
    frac_in,
    wexp,
    b3_in,
    out,
    fv,
    x1,
    w1,
    b1,
    w2,
    b2,
    req,
    slot,
    frac,
    b3,
    h1,
    e1s,
    e1r,
    e2s,
    e2r,
    acc_edge,
    oha,
    ohb,
    sa,
    sb,
    keyt,
    wt,
    reqt,
    reqg,
    pbuf,
    arr,
    h2t,
    rq,
    wr,
    wx,
    rbuf,
    in_sem,
    e1_send,
    e1_recv,
    e2_send,
    e2_recv,
    rq_send,
    rq_recv,
    rg_send,
    rg_recv,
    w_send,
    w_recv,
    g_send,
    g_recv,
    r_send,
    r_recv,
    a_send,
    a_recv,
):
    az = lax.axis_index("az")
    ch = lax.axis_index("ch")
    nz, nx, ny = torus(n)
    members = nx * ny
    groups = nz
    chans = x1.shape[0] // 4
    ranges = x1.shape[1]
    outs = w1.shape[0] // 9
    cart = slot.shape[1]
    rows = members * HALF
    hh = out.shape[0]
    share = n // 4
    right = lax.rem(az + 1, n)
    left = lax.rem(az + n - 1, n)
    my_z = az // members
    my_x = lax.rem(az, members) // ny
    my_y = lax.rem(az, ny)

    barrier = pltpu.get_barrier_semaphore()

    def greet(d, _):
        to = az + d
        pl.semaphore_signal(
            barrier,
            inc=1,
            device_id=(jnp.where(to >= n, to - n, to), ch),
            device_id_type=MESH,
        )
        return 0

    lax.fori_loop(1, n, greet, 0, unroll=True)
    for d in range(1, 4):
        pl.semaphore_signal(
            barrier, inc=1, device_id=(az, lax.rem(ch + d, 4)), device_id_type=MESH
        )

    fetches = []
    pairs = (
        (feat, fv),
        (w1_in, w1),
        (req_in, req),
        (b1_in, b1),
        (w2_in, w2),
        (b2_in, b2),
        (slot_in, slot),
        (frac_in, frac),
        (b3_in, b3),
    )
    for k, (src, dst) in enumerate(pairs):
        c = pltpu.make_async_copy(src, dst, in_sem.at[k])
        c.start()
        fetches.append(c)

    def at_column(col):
        return slice(col * chans, (col + 1) * chans)

    def part(w, x, col):
        total = None
        for tap in range(3):
            src = col + tap - 1
            if 0 <= src <= 3:
                term = jnp.dot(
                    w[tap * 3 * outs : (tap + 1) * 3 * outs, :],
                    x[at_column(src), :],
                    preferred_element_type=F32,
                )
                total = term if total is None else total + term
        return combine(total, outs, ranges)

    fetches[0].wait()
    for col in range(4):
        x1[at_column(col), :] = fv[:, col, :]
    fetches[1].wait()
    e1s[0] = part(w1, x1, 4).astype(BF)
    e1s[1] = part(w1, x1, -1).astype(BF)
    fetches[2].wait()

    pl.semaphore_wait(barrier, n + 2)

    def edge(src, dst, send, recv):
        copies = []
        for k, to in ((0, right), (1, left)):
            copies.append(
                pltpu.make_async_remote_copy(
                    src_ref=src.at[k],
                    dst_ref=dst.at[k],
                    send_sem=send.at[k],
                    recv_sem=recv.at[k],
                    device_id=(to, ch),
                    device_id_type=MESH,
                )
            )
        return copies

    e1 = edge(e1s, e1r, e1_send, e1_recv)
    for c in e1:
        c.start()

    def shifted(g, i, sign):
        dz = lax.rem(g + i, nz)
        dx = i // ny
        dy = lax.rem(i, ny)
        if sign > 0:
            z, x, y = my_z + dz, my_x + dx, my_y + dy
        else:
            z, x, y = my_z + nz - dz, my_x + nx - dx, my_y + ny - dy
        return lax.rem(z, nz) * members + lax.rem(x, nx) * ny + lax.rem(y, ny)

    def ask(k, _):
        p = ch * share + k
        to = shifted(p // members, lax.rem(p, members), -1)
        pltpu.make_async_remote_copy(
            src_ref=req.at[to // 4],
            dst_ref=rq.at[p],
            send_sem=rq_send,
            recv_sem=rq_recv,
            device_id=(to, ch),
            device_id_type=MESH,
        ).start()
        return 0

    @pl.when(ch == 0)
    def _():
        pltpu.make_async_copy(req.at[az // 4], rq.at[0], rq_recv).start()

    lax.fori_loop(jnp.where(ch == 0, 1, 0), share, ask, 0)

    wcopies = []
    for d in range(1, 4):
        to = lax.rem(ch + d, 4)
        c = pltpu.make_async_remote_copy(
            src_ref=wexp.at[:, pl.ds(pl.multiple_of(to * hh, hh), hh)],
            dst_ref=wr.at[ch],
            send_sem=w_send.at[d - 1],
            recv_sem=w_recv.at[d - 1],
            device_id=(az, to),
            device_id_type=MESH,
        )
        c.start()
        wcopies.append(c)
    own_w = pltpu.make_async_copy(
        wexp.at[:, pl.ds(pl.multiple_of(ch * hh, hh), hh)], wr.at[ch], in_sem.at[len(pairs)]
    )
    own_w.start()

    fetches[3].wait()
    bias1 = column_of(b1[...])

    def mine(col):
        return pl.ds(pl.multiple_of(col * chans + ch * outs, outs), outs)

    def spread(col):
        copies = []
        for d in range(1, 4):
            c = pltpu.make_async_remote_copy(
                src_ref=h1.at[mine(col)],
                dst_ref=h1.at[mine(col)],
                send_sem=g_send.at[col, d - 1],
                recv_sem=g_recv.at[col, d - 1],
                device_id=(az, lax.rem(ch + d, 4)),
                device_id_type=MESH,
            )
            c.start()
            copies.append(c)
        return copies

    gathers = {}
    for col in (1, 2):
        h1[mine(col), :] = jnp.maximum(part(w1, x1, col) + bias1, 0.0).astype(BF)
        gathers[col] = spread(col)
    for k, col in ((0, 0), (1, 3)):
        acc_edge[k] = part(w1, x1, col) + bias1

    def asked(ref, at, count, send, recv):
        return pltpu.make_async_remote_copy(
            src_ref=ref.at[pl.ds(at, count)],
            dst_ref=ref.at[pl.ds(at, count)],
            send_sem=send,
            recv_sem=recv,
            device_id=(right, ch),
            device_id_type=MESH,
        )

    asked(rq, 0, share, rq_send, rq_recv).wait_recv()
    passed = []
    for d in range(1, 4):
        at = pl.ds(pl.multiple_of(ch * share, share), share)
        c = pltpu.make_async_remote_copy(
            src_ref=rq.at[at],
            dst_ref=rq.at[at],
            send_sem=rg_send.at[d - 1],
            recv_sem=rg_recv.at[d - 1],
            device_id=(az, lax.rem(ch + d, 4)),
            device_id_type=MESH,
        )
        passed.append(c)

    for k, col in ((0, 0), (1, 3)):
        e1[k].wait_recv()
        h1[mine(col), :] = jnp.maximum(acc_edge[k] + e1r[k].astype(F32), 0.0).astype(BF)
        gathers[col] = spread(col)
    for c in passed:
        c.start()

    for c in fetches[4:]:
        c.wait()
    q = slot[...]
    sector = lax.shift_right_logical(q, 5)
    low = jnp.bitwise_and(q, HALF - 1)
    upper = jnp.bitwise_and(q, HALF) != 0
    dx = jnp.bitwise_and(my_x - jnp.bitwise_and(sector // ny, nx - 1), nx - 1)
    dy = jnp.bitwise_and(my_y - jnp.bitwise_and(sector, ny - 1), ny - 1)
    place_i = dx * ny + dy
    place_g = jnp.bitwise_and(my_z - sector // members - place_i, nz - 1)
    m = (place_g * members + place_i) * HALF + low
    keys = jnp.concatenate(
        [jnp.where(upper, -1, m), jnp.where(upper, m, -1)]
        + [jnp.zeros((120, cart), jnp.int32)],
        axis=0,
    )
    keyt[...] = keys.T
    u, v = frac[0:1, :], frac[1:2, :]
    weights = jnp.concatenate(
        [(1.0 - u) * (1.0 - v), u * (1.0 - v), (1.0 - u) * v, u * v]
        + [jnp.zeros((124, cart), F32)],
        axis=0,
    )
    wt[...] = weights.T
    width = min(128, n * HALF)

    def s_rows(b, _):
        at = pl.ds(pl.multiple_of(b * 16, 16), 16)
        spot = lax.broadcasted_iota(jnp.int32, (16, width), 1).astype(jnp.int16)
        parts = [jnp.broadcast_to(wt[at, k : k + 1], (16, width)).astype(BF) for k in range(4)]
        for base, ref in ((0, sa), (4, sb)):
            found = [
                jnp.broadcast_to(keyt[at, base + k : base + k + 1], (16, width)).astype(jnp.int16)
                for k in range(4)
            ]
            for j in range(n * HALF // width):
                here = spot + jnp.int16(j * width)
                total = jnp.zeros((16, width), BF)
                for k in range(4):
                    total = jnp.where(here == found[k], parts[k], total)
                ref[at, j * width : (j + 1) * width] = total
        return 0

    lax.fori_loop(0, cart // 16, s_rows, 0, unroll=2 if cart >= 32 else 1)

    for col in (3, 0):
        for c in gathers[col]:
            c.wait_recv()
    e2s[0] = part(w2, h1, 4).astype(BF)
    e2s[1] = part(w2, h1, -1).astype(BF)
    e2 = edge(e2s, e2r, e2_send, e2_recv)
    for c in e2:
        c.start()
    for col in (1, 2):
        for c in gathers[col]:
            c.wait_recv()

    def place(col, value):
        zero = jnp.zeros((128 - outs, ranges), F32)
        at = slice(col * ranges, (col + 1) * ranges)
        h2t[0, at, :] = jnp.concatenate([value, zero], axis=0).T.astype(BF)
        h2t[1, at, :] = jnp.concatenate([zero, value], axis=0).T.astype(BF)

    bias2 = column_of(b2[...])
    for col in (1, 2):
        place(col, jnp.maximum(part(w2, h1, col) + bias2, 0.0))
    for k, col in ((0, 0), (1, 3)):
        acc_edge[k] = part(w2, h1, col) + bias2

    for c in passed:
        c.wait_recv()
    reqt[...] = rq[:, 0, :].T
    wanted = reqt[pl.ds(pl.multiple_of(lax.rem(az, 4) * 2 * HALF, 2 * HALF), 2 * HALF), :]
    for g in range(groups):
        reqg[g] = wanted[:, g * members : (g + 1) * members]

    def one_hot(g, _):
        some = reqg[g]
        spot = lax.broadcasted_iota(jnp.int32, (HALF, 4 * ranges), 1)
        for i in range(members):
            at = pl.ds(pl.multiple_of(g * rows + i * HALF, HALF), HALF)
            oha[at, :] = jnp.where(spot == some[:HALF, i : i + 1], 1.0, 0.0).astype(BF)
            ohb[at, :] = jnp.where(spot == some[HALF:, i : i + 1], 1.0, 0.0).astype(BF)
        return 0

    lax.fori_loop(0, groups, one_hot, 0)

    own_w.wait()
    for d in range(3):
        wcopies[d].wait_recv()
    for g in range(4):
        block = wr[g].astype(F32)
        zero = jnp.zeros((128 - outs, hh), F32)
        wx[0, :, g * 128 : (g + 1) * 128] = jnp.concatenate([block, zero], axis=0).T.astype(BF)
        wx[1, :, g * 128 : (g + 1) * 128] = jnp.concatenate([zero, block], axis=0).T.astype(BF)
    bias3 = column_of(b3[...])

    for k, col in ((0, 0), (1, 3)):
        e2[k].wait_recv()
        place(col, jnp.maximum(acc_edge[k] + e2r[k].astype(F32), 0.0))

    for g in range(groups):
        at = slice(g * rows, (g + 1) * rows)
        picked = jnp.dot(oha[at, :], h2t[0], preferred_element_type=F32)
        picked += jnp.dot(ohb[at, :], h2t[1], preferred_element_type=F32)
        pbuf[g] = picked.astype(BF)

        def ship(i, _):
            block = pl.ds(pl.multiple_of(i * HALF, HALF), HALF)
            pltpu.make_async_remote_copy(
                src_ref=pbuf.at[g, block],
                dst_ref=arr.at[g, block],
                send_sem=a_send.at[g],
                recv_sem=a_recv.at[g],
                device_id=(shifted(g, i, 1), ch),
                device_id_type=MESH,
            ).start()
            return 0

        lax.fori_loop(1 if g == 0 else 0, members, ship, 0)
        if g == 0:
            arr[0, :HALF, :] = pbuf[0, :HALF, :]

    def whole(g):
        size = rows - HALF if g == 0 else rows
        return pltpu.make_async_remote_copy(
            src_ref=pbuf.at[g, pl.ds(0, size)],
            dst_ref=arr.at[g, pl.ds(0, size)],
            send_sem=a_send.at[g],
            recv_sem=a_recv.at[g],
            device_id=(right, ch),
            device_id_type=MESH,
        )

    total_a = jnp.zeros((cart, 128), F32)
    total_b = jnp.zeros((cart, 128), F32)
    for g in range(groups):
        whole(g).wait_recv()
        at = slice(g * rows, (g + 1) * rows)
        total_a += jnp.dot(sa[:, at], arr[g], preferred_element_type=F32)
        total_b += jnp.dot(sb[:, at], arr[g], preferred_element_type=F32)

    half = cart // 2
    lane = lax.broadcasted_iota(jnp.int32, (half, 128), 1)
    first = total_a[:half] + pltpu.roll(total_b[:half], 64, 1)
    second = pltpu.roll(total_a[half:], 64, 1) + total_b[half:]
    rbuf[ch] = jnp.where(lane < 64, first, second).astype(BF)
    rcopies = []
    for d in range(1, 4):
        c = pltpu.make_async_remote_copy(
            src_ref=rbuf.at[ch],
            dst_ref=rbuf.at[ch],
            send_sem=r_send.at[d - 1],
            recv_sem=r_recv.at[d - 1],
            device_id=(az, lax.rem(ch + d, 4)),
            device_id_type=MESH,
        )
        c.start()
        rcopies.append(c)
    for c in rcopies:
        c.wait_recv()
    for p in range(2):
        sum_p = jnp.zeros((hh, half), F32)
        for g in range(4):
            sum_p += lax.dot_general(
                wx[p, :, g * 128 : (g + 1) * 128],
                rbuf[g],
                (((1,), (1,)), ((), ())),
                preferred_element_type=F32,
            )
        out[:, p * half : (p + 1) * half] = (sum_p + bias3).astype(BF)

    for c in e1 + e2 + wcopies + passed + rcopies + [c for k in range(4) for c in gathers[k]]:
        c.wait_send()

    @pl.when(ch == 0)
    def _():
        asked(rq, 0, share - 1, rq_send, rq_recv).wait_send()

    @pl.when(ch != 0)
    def _():
        asked(rq, 0, share, rq_send, rq_recv).wait_send()

    for g in range(groups):
        whole(g).wait_send()


def local(
    features,
    conv1_weight,
    conv1_bias,
    conv2_weight,
    conv2_bias,
    request_cell,
    corner_slot,
    corner_frac,
    expand_weight,
    expand_bias,
):
    n = lax.axis_size("az")
    chans, columns, ranges = features.shape
    outs = conv1_weight.shape[0]
    cart = corner_slot.shape[1]
    hh = expand_bias.shape[0]
    groups = torus(n)[0]
    members = n // groups
    rows = members * HALF

    w1 = conv1_weight.transpose(1, 2, 0, 3).reshape(9 * outs, chans)
    w2 = conv2_weight.transpose(1, 2, 0, 3).reshape(9 * outs, chans)
    args = (
        features,
        w1,
        conv1_bias.reshape(1, outs),
        w2,
        conv2_bias.reshape(1, outs),
        request_cell.reshape(n * 2 * HALF // 128, 1, 128),
        corner_slot,
        corner_frac,
        expand_weight,
        expand_bias.reshape(1, hh),
    )
    dma = pltpu.SemaphoreType.DMA
    return pl.pallas_call(
        functools.partial(kernel, n),
        out_shape=jax.ShapeDtypeStruct((hh, cart), BF),
        in_specs=[pl.BlockSpec(memory_space=pl.ANY)] * len(args),
        out_specs=pl.BlockSpec(memory_space=pltpu.VMEM),
        scratch_shapes=[
            pltpu.VMEM((chans, 4, ranges), BF),
            pltpu.VMEM((4 * chans, ranges), BF),
            pltpu.VMEM((9 * outs, chans), BF),
            pltpu.VMEM((1, outs), F32),
            pltpu.VMEM((9 * outs, chans), BF),
            pltpu.VMEM((1, outs), F32),
            pltpu.VMEM((n * 2 * HALF // 128, 1, 128), jnp.int32),
            pltpu.VMEM((4, cart), jnp.int32),
            pltpu.VMEM((2, cart), F32),
            pltpu.VMEM((1, hh), F32),
            pltpu.VMEM((4 * chans, ranges), BF),
            pltpu.VMEM((2, outs, ranges), BF),
            pltpu.VMEM((2, outs, ranges), BF),
            pltpu.VMEM((2, outs, ranges), BF),
            pltpu.VMEM((2, outs, ranges), BF),
            pltpu.VMEM((2, outs, ranges), F32),
            pltpu.VMEM((n * HALF, 4 * ranges), BF),
            pltpu.VMEM((n * HALF, 4 * ranges), BF),
            pltpu.VMEM((cart, n * HALF), BF),
            pltpu.VMEM((cart, n * HALF), BF),
            pltpu.VMEM((cart, 128), jnp.int32),
            pltpu.VMEM((cart, 128), F32),
            pltpu.VMEM((128, n), jnp.int32),
            pltpu.VMEM((groups, 2 * HALF, members), jnp.int32),
            pltpu.VMEM((groups, rows, 128), BF),
            pltpu.VMEM((groups, rows, 128), BF),
            pltpu.VMEM((2, 4 * ranges, 128), BF),
            pltpu.VMEM((n, 1, 128), jnp.int32),
            pltpu.VMEM((4, outs, hh), BF),
            pltpu.VMEM((2, hh, 512), BF),
            pltpu.VMEM((4, cart // 2, 128), BF),
            dma((10,)),
            dma((2,)),
            dma((2,)),
            dma((2,)),
            dma((2,)),
            dma,
            dma,
            dma((3,)),
            dma((3,)),
            dma((3,)),
            dma((3,)),
            dma((4, 3)),
            dma((4, 3)),
            dma((3,)),
            dma((3,)),
            dma((groups,)),
            dma((groups,)),
        ],
        compiler_params=pltpu.CompilerParams(
            collective_id=0, has_side_effects=True, vmem_limit_bytes=60 * 1024 * 1024
        ),
        cost_estimate=pl.CostEstimate(
            flops=4 * 10**9, bytes_accessed=2 * 10**6, transcendentals=0
        ),
    )(*args)


def solution(mesh):
    return jax.shard_map(
        local,
        mesh=mesh,
        in_specs=(
            P(None, "az", None),
            P("ch", None, None, None),
            P("ch"),
            P("ch", None, None, None),
            P("ch"),
            P("az"),
            P(None, "az"),
            P(None, "az"),
            P("ch", None),
            P("ch"),
        ),
        out_specs=P("ch", "az"),
        check_vma=False,
    )
```

time: 81.7 us -> 61.1 us (0.75)
  Pallas kernels: 75.9 us -> 59.4 us
  local copies, waits for them, and re-layouts: 5.45 us -> 1.57 us
    pallas_call x1, Pallas kernels: 75.9 us -> 59.4 us  [local(): pl.pallas_call(functools.partial(kernel, n), out_shape=jax.ShapeDtypeStru...]
    transpose x4 -> x0, local copies, waits for them, and re-layouts: 1.56 us -> none  [the longest x1 1.22 us: local(): w1 = conv1_weight.transpose(2, 0, 1, 3).reshape(3 * outs, 3 * chans)]
    unnamed x19 -> x1, local copies, waits for them, and re-layouts: 3.07 us -> 1.57 us
    reshape x1 -> x0, local copies, waits for them, and re-layouts: 0.82 us -> none  [local(): request_cell.reshape(n, 1, 2 * HALF)]
where the time goes in v2:
time: 61.1 us; the launch traced here: 61 us
  Pallas kernels  59.4 us (97%)
  local copies, waits for them, and re-layouts  1.57 us (3%)
    pallas_call x1, Pallas kernels, local(): pl.pallas_call(functools.partial(kernel, n), out_shape=jax.ShapeDtypeStru...  59.4 us
    unnamed x1, local copies, waits for them, and re-layouts  1.57 us

profile of v2, /device:TPU:1, one launch (start us, length us, event | category | flops | bytes accessed | tf_op | source)
XLA Modules:
  0.0 61.0 jit_solution(7069704433231138360)
XLA Ops:
  0.0 59.4 %shard_map.100 = bf16[128,512]{1,0:T(8,128)(2,1)} custom-call(bf16[256,4,256]{2,1,0:T(4,128)(2,1)} %feat.1, bf16[576,256]{1,0:T(8,128)(2,1)} %bitcast.10, f32[1,64]{1,0:T(1,128)} %bitcast.13, bf16[576,256]{1,0:T(8,128)(2,1)} %bitcast.11, f32[1,64]{1,0:T(1,128)} %bitcast.14, s32[32,1,128]{2,1,0:T(1,128)} %bitcast.12, s32[4,512]{1,0:T(4,128)} %slot_in.1, ...), custom_call_target="tpu_custom_call" | custom-call | flops 4000000000 | bytes 2000000 | tf_op jit(solution)/shard_map/pallas_call | solution.py:523
  59.4 1.6 %copy.12 = bf16[128,512]{1,0:T(8,128)(2,1)} copy(bf16[128,512]{1,0:T(8,128)(2,1)} %shard_map.100) | data formatting | bytes 262144

commit v3 on v2

--- a/solution.py
+++ b/solution.py
@@ -111,24 +111,6 @@
     my_x = lax.rem(az, members) // ny
     my_y = lax.rem(az, ny)
 
-    barrier = pltpu.get_barrier_semaphore()
-
-    def greet(d, _):
-        to = az + d
-        pl.semaphore_signal(
-            barrier,
-            inc=1,
-            device_id=(jnp.where(to >= n, to - n, to), ch),
-            device_id_type=MESH,
-        )
-        return 0
-
-    lax.fori_loop(1, n, greet, 0, unroll=True)
-    for d in range(1, 4):
-        pl.semaphore_signal(
-            barrier, inc=1, device_id=(az, lax.rem(ch + d, 4)), device_id_type=MESH
-        )
-
     fetches = []
     pairs = (
         (feat, fv),
@@ -146,6 +128,30 @@
         c.start()
         fetches.append(c)
 
+    side, core = ch // 2, lax.rem(ch, 2)
+    peers = {
+        1: side * 2 + 1 - core,
+        2: (1 - side) * 2 + core,
+        3: (1 - side) * 2 + 1 - core,
+    }
+
+    barrier = pltpu.get_barrier_semaphore()
+
+    def hail(to_az, to_ch):
+        pl.semaphore_signal(barrier, inc=1, device_id=(to_az, to_ch), device_id_type=MESH)
+
+    hail(right, ch)
+    hail(left, ch)
+    for d in range(1, 4):
+        hail(az, peers[d])
+
+    def greet(d, _):
+        to = az + d
+        hail(jnp.where(to >= n, to - n, to), ch)
+        return 0
+
+    lax.fori_loop(2, n - 1, greet, 0, unroll=True)
+
     def at_column(col):
         return slice(col * chans, (col + 1) * chans)
 
@@ -163,7 +169,7 @@
         return combine(total, outs, ranges)
 
     fetches[0].wait()
-    for col in range(4):
+    for col in (3, 0):
         x1[at_column(col), :] = fv[:, col, :]
     fetches[1].wait()
     e1s[0] = part(w1, x1, 4).astype(BF)
@@ -222,7 +228,7 @@
 
     wcopies = []
     for d in range(1, 4):
-        to = lax.rem(ch + d, 4)
+        to = peers[d]
         c = pltpu.make_async_remote_copy(
             src_ref=wexp.at[:, pl.ds(pl.multiple_of(to * hh, hh), hh)],
             dst_ref=wr.at[ch],
@@ -238,32 +244,34 @@
     )
     own_w.start()
 
+    for col in (1, 2):
+        x1[at_column(col), :] = fv[:, col, :]
     fetches[3].wait()
     bias1 = column_of(b1[...])
 
     def mine(col):
         return pl.ds(pl.multiple_of(col * chans + ch * outs, outs), outs)
 
-    def spread(col):
-        copies = []
-        for d in range(1, 4):
-            c = pltpu.make_async_remote_copy(
-                src_ref=h1.at[mine(col)],
-                dst_ref=h1.at[mine(col)],
-                send_sem=g_send.at[col, d - 1],
-                recv_sem=g_recv.at[col, d - 1],
-                device_id=(az, lax.rem(ch + d, 4)),
-                device_id_type=MESH,
-            )
-            c.start()
-            copies.append(c)
-        return copies
+    def block_of(col, owner):
+        return pl.ds(pl.multiple_of(col * chans + owner * outs, outs), outs)
+
+    def pass_block(col, owner, to, lane):
+        c = pltpu.make_async_remote_copy(
+            src_ref=h1.at[block_of(col, owner)],
+            dst_ref=h1.at[block_of(col, owner)],
+            send_sem=g_send.at[col, lane - 1],
+            recv_sem=g_recv.at[col, lane - 1],
+            device_id=(az, peers[to]),
+            device_id_type=MESH,
+        )
+        c.start()
+        return c
 
     gathers = {}
     for col in (1, 2):
         h1[mine(col), :] = jnp.maximum(part(w1, x1, col) + bias1, 0.0).astype(BF)
-        gathers[col] = spread(col)
-    for k, col in ((0, 0), (1, 3)):
+        gathers[col] = [pass_block(col, ch, d, d) for d in (2, 1)]
+    for k, col in ((1, 3), (0, 0)):
         acc_edge[k] = part(w1, x1, col) + bias1
 
     def asked(ref, at, count, send, recv):
@@ -276,6 +284,14 @@
             device_id_type=MESH,
         )
 
+    for k, col in ((1, 3), (0, 0)):
+        e1[k].wait_recv()
+        h1[mine(col), :] = jnp.maximum(acc_edge[k] + e1r[k].astype(F32), 0.0).astype(BF)
+        gathers[col] = [pass_block(col, ch, d, d) for d in (3, 2, 1)]
+    for col in (1, 2):
+        gathers[col][0].wait_recv()
+        gathers[col].append(pass_block(col, peers[2], 1, 3))
+
     asked(rq, 0, share, rq_send, rq_recv).wait_recv()
     passed = []
     for d in range(1, 4):
@@ -285,17 +301,11 @@
             dst_ref=rq.at[at],
             send_sem=rg_send.at[d - 1],
             recv_sem=rg_recv.at[d - 1],
-            device_id=(az, lax.rem(ch + d, 4)),
+            device_id=(az, peers[d]),
             device_id_type=MESH,
         )
+        c.start()
         passed.append(c)
-
-    for k, col in ((0, 0), (1, 3)):
-        e1[k].wait_recv()
-        h1[mine(col), :] = jnp.maximum(acc_edge[k] + e1r[k].astype(F32), 0.0).astype(BF)
-        gathers[col] = spread(col)
-    for c in passed:
-        c.start()
 
     for c in fetches[4:]:
         c.wait()
@@ -342,17 +352,16 @@
 
     lax.fori_loop(0, cart // 16, s_rows, 0, unroll=2 if cart >= 32 else 1)
 
-    for col in (3, 0):
+    e2 = edge(e2s, e2r, e2_send, e2_recv)
+    for k, col, to in ((0, 3, 4), (1, 0, -1)):
         for c in gathers[col]:
             c.wait_recv()
-    e2s[0] = part(w2, h1, 4).astype(BF)
-    e2s[1] = part(w2, h1, -1).astype(BF)
-    e2 = edge(e2s, e2r, e2_send, e2_recv)
-    for c in e2:
-        c.start()
-    for col in (1, 2):
-        for c in gathers[col]:
-            c.wait_recv()
+        e2s[k] = part(w2, h1, to).astype(BF)
+        e2[k].start()
+    gathers[1][1].wait_recv()
+    gathers[1][2].wait_recv()
+    gathers[2][1].wait_recv()
+    gathers[2][2].wait_recv()
 
     def place(col, value):
         zero = jnp.zeros((128 - outs, ranges), F32)
@@ -451,7 +460,7 @@
             dst_ref=rbuf.at[ch],
             send_sem=r_send.at[d - 1],
             recv_sem=r_recv.at[d - 1],
-            device_id=(az, lax.rem(ch + d, 4)),
+            device_id=(az, peers[d]),
             device_id_type=MESH,
         )
         c.start()

time: 61.1 us -> 59.3 us (0.971)
  Pallas kernels: 59.4 us -> 57.6 us
    pallas_call x1, Pallas kernels: 59.4 us -> 57.6 us  [local(): pl.pallas_call(functools.partial(kernel, n), out_shape=jax.ShapeDtypeStru...]
where the time goes in v3:
time: 59.3 us; the launch traced here: 59.2 us
  Pallas kernels  57.6 us (97%)
  local copies, waits for them, and re-layouts  1.57 us (3%)
    pallas_call x1, Pallas kernels, local(): pl.pallas_call(functools.partial(kernel, n), out_shape=jax.ShapeDtypeStru...  57.6 us
    unnamed x1, local copies, waits for them, and re-layouts  1.57 us

profile of v3, /device:TPU:1, one launch (start us, length us, event | category | flops | bytes accessed | tf_op | source)
XLA Modules:
  0.0 59.2 jit_solution(8840032463427327278)
XLA Ops:
  0.0 57.6 %shard_map.100 = bf16[128,512]{1,0:T(8,128)(2,1)} custom-call(bf16[256,4,256]{2,1,0:T(4,128)(2,1)} %feat.1, bf16[576,256]{1,0:T(8,128)(2,1)} %bitcast.10, f32[1,64]{1,0:T(1,128)} %bitcast.13, bf16[576,256]{1,0:T(8,128)(2,1)} %bitcast.11, f32[1,64]{1,0:T(1,128)} %bitcast.14, s32[32,1,128]{2,1,0:T(1,128)} %bitcast.12, s32[4,512]{1,0:T(4,128)} %slot_in.1, ...), custom_call_target="tpu_custom_call" | custom-call | flops 4000000000 | bytes 2000000 | tf_op jit(solution)/shard_map/pallas_call | solution.py:532
  57.6 1.6 %copy.12 = bf16[128,512]{1,0:T(8,128)(2,1)} copy(bf16[128,512]{1,0:T(8,128)(2,1)} %shard_map.100) | data formatting | bytes 262144

commit v4 on v3

--- a/solution.py
+++ b/solution.py
@@ -197,19 +197,24 @@
     for c in e1:
         c.start()
 
-    def shifted(g, i, sign):
-        dz = lax.rem(g + i, nz)
-        dx = i // ny
-        dy = lax.rem(i, ny)
-        if sign > 0:
-            z, x, y = my_z + dz, my_x + dx, my_y + dy
+    ahead_z = [lax.rem(my_z + d, nz) * members for d in range(nz)]
+    back_z = [lax.rem(my_z + nz - d, nz) * members for d in range(nz)]
+    ahead_xy, back_xy = [], []
+    for i in range(members):
+        ix, iy = i // ny, i % ny
+        ahead_xy.append(lax.rem(my_x + ix, nx) * ny + lax.rem(my_y + iy, ny))
+        back_xy.append(lax.rem(my_x + nx - ix, nx) * ny + lax.rem(my_y + ny - iy, ny))
+
+    def ask(k):
+        p = ch * share + k
+        g = p // members
+        i = lax.rem(p, members) if share % members else k % members
+        if share % members:
+            ix, iy = i // ny, lax.rem(i, ny)
+            xy = lax.rem(my_x + nx - ix, nx) * ny + lax.rem(my_y + ny - iy, ny)
         else:
-            z, x, y = my_z + nz - dz, my_x + nx - dx, my_y + ny - dy
-        return lax.rem(z, nz) * members + lax.rem(x, nx) * ny + lax.rem(y, ny)
-
-    def ask(k, _):
-        p = ch * share + k
-        to = shifted(p // members, lax.rem(p, members), -1)
+            xy = back_xy[i]
+        to = lax.rem(my_z + nz - lax.rem(g + i, nz), nz) * members + xy
         pltpu.make_async_remote_copy(
             src_ref=req.at[to // 4],
             dst_ref=rq.at[p],
@@ -218,13 +223,6 @@
             device_id=(to, ch),
             device_id_type=MESH,
         ).start()
-        return 0
-
-    @pl.when(ch == 0)
-    def _():
-        pltpu.make_async_copy(req.at[az // 4], rq.at[0], rq_recv).start()
-
-    lax.fori_loop(jnp.where(ch == 0, 1, 0), share, ask, 0)
 
     wcopies = []
     for d in range(1, 4):
@@ -244,6 +242,17 @@
     )
     own_w.start()
 
+    @pl.when(ch == 0)
+    def _():
+        pltpu.make_async_copy(req.at[az // 4], rq.at[0], rq_recv).start()
+
+    @pl.when(ch != 0)
+    def _():
+        ask(0)
+
+    for k in range(1, share):
+        ask(k)
+
     for col in (1, 2):
         x1[at_column(col), :] = fv[:, col, :]
     fetches[3].wait()
@@ -291,6 +300,19 @@
     for col in (1, 2):
         gathers[col][0].wait_recv()
         gathers[col].append(pass_block(col, peers[2], 1, 3))
+
+    own_w.wait()
+    for d in range(3):
+        wcopies[d].wait_recv()
+    for g in range(4):
+        block = wr[g].astype(F32)
+        zero = jnp.zeros((128 - outs, hh), F32)
+        wx[0, :, g * 128 : (g + 1) * 128] = jnp.concatenate([block, zero], axis=0).T.astype(BF)
+        wx[1, :, g * 128 : (g + 1) * 128] = jnp.concatenate([zero, block], axis=0).T.astype(BF)
+    for k in (4, 5, 8):
+        fetches[k].wait()
+    bias2 = column_of(b2[...])
+    bias3 = column_of(b3[...])
 
     asked(rq, 0, share, rq_send, rq_recv).wait_recv()
     passed = []
@@ -307,8 +329,71 @@
         c.start()
         passed.append(c)
 
-    for c in fetches[4:]:
-        c.wait()
+    e2 = edge(e2s, e2r, e2_send, e2_recv)
+    for k, col, to in ((0, 3, 4), (1, 0, -1)):
+        for c in gathers[col]:
+            c.wait_recv()
+        e2s[k] = part(w2, h1, to).astype(BF)
+        e2[k].start()
+    gathers[1][1].wait_recv()
+    gathers[1][2].wait_recv()
+    gathers[2][1].wait_recv()
+    gathers[2][2].wait_recv()
+
+    def place(col, value):
+        zero = jnp.zeros((128 - outs, ranges), F32)
+        at = slice(col * ranges, (col + 1) * ranges)
+        h2t[0, at, :] = jnp.concatenate([value, zero], axis=0).T.astype(BF)
+        h2t[1, at, :] = jnp.concatenate([zero, value], axis=0).T.astype(BF)
+
+    for col in (1, 2):
+        place(col, jnp.maximum(part(w2, h1, col) + bias2, 0.0))
+    for k, col in ((0, 0), (1, 3)):
+        acc_edge[k] = part(w2, h1, col) + bias2
+
+    for c in passed:
+        c.wait_recv()
+    reqt[...] = rq[:, 0, :].T
+    wanted = reqt[pl.ds(pl.multiple_of(lax.rem(az, 4) * 2 * HALF, 2 * HALF), 2 * HALF), :]
+    for g in range(groups):
+        reqg[g] = wanted[:, g * members : (g + 1) * members]
+
+    def one_hot(g, _):
+        some = reqg[g]
+        spot = lax.broadcasted_iota(jnp.int32, (HALF, 4 * ranges), 1)
+        for i in range(members):
+            at = pl.ds(pl.multiple_of(g * rows + i * HALF, HALF), HALF)
+            oha[at, :] = jnp.where(spot == some[:HALF, i : i + 1], 1.0, 0.0).astype(BF)
+            ohb[at, :] = jnp.where(spot == some[HALF:, i : i + 1], 1.0, 0.0).astype(BF)
+        return 0
+
+    lax.fori_loop(0, groups, one_hot, 0)
+
+    for k, col in ((0, 0), (1, 3)):
+        e2[k].wait_recv()
+        place(col, jnp.maximum(acc_edge[k] + e2r[k].astype(F32), 0.0))
+
+    for g in range(groups):
+        at = slice(g * rows, (g + 1) * rows)
+        picked = jnp.dot(oha[at, :], h2t[0], preferred_element_type=F32)
+        picked += jnp.dot(ohb[at, :], h2t[1], preferred_element_type=F32)
+        pbuf[g] = picked.astype(BF)
+
+        for i in range(1 if g == 0 else 0, members):
+            block = slice(i * HALF, (i + 1) * HALF)
+            pltpu.make_async_remote_copy(
+                src_ref=pbuf.at[g, block],
+                dst_ref=arr.at[g, block],
+                send_sem=a_send.at[g],
+                recv_sem=a_recv.at[g],
+                device_id=(ahead_z[(g + i) % nz] + ahead_xy[i], ch),
+                device_id_type=MESH,
+            ).start()
+        if g == 0:
+            arr[0, :HALF, :] = pbuf[0, :HALF, :]
+
+    fetches[6].wait()
+    fetches[7].wait()
     q = slot[...]
     sector = lax.shift_right_logical(q, 5)
     low = jnp.bitwise_and(q, HALF - 1)
@@ -352,83 +437,6 @@
 
     lax.fori_loop(0, cart // 16, s_rows, 0, unroll=2 if cart >= 32 else 1)
 
-    e2 = edge(e2s, e2r, e2_send, e2_recv)
-    for k, col, to in ((0, 3, 4), (1, 0, -1)):
-        for c in gathers[col]:
-            c.wait_recv()
-        e2s[k] = part(w2, h1, to).astype(BF)
-        e2[k].start()
-    gathers[1][1].wait_recv()
-    gathers[1][2].wait_recv()
-    gathers[2][1].wait_recv()
-    gathers[2][2].wait_recv()
-
-    def place(col, value):
-        zero = jnp.zeros((128 - outs, ranges), F32)
-        at = slice(col * ranges, (col + 1) * ranges)
-        h2t[0, at, :] = jnp.concatenate([value, zero], axis=0).T.astype(BF)
-        h2t[1, at, :] = jnp.concatenate([zero, value], axis=0).T.astype(BF)
-
-    bias2 = column_of(b2[...])
-    for col in (1, 2):
-        place(col, jnp.maximum(part(w2, h1, col) + bias2, 0.0))
-    for k, col in ((0, 0), (1, 3)):
-        acc_edge[k] = part(w2, h1, col) + bias2
-
-    for c in passed:
-        c.wait_recv()
-    reqt[...] = rq[:, 0, :].T
-    wanted = reqt[pl.ds(pl.multiple_of(lax.rem(az, 4) * 2 * HALF, 2 * HALF), 2 * HALF), :]
-    for g in range(groups):
-        reqg[g] = wanted[:, g * members : (g + 1) * members]
-
-    def one_hot(g, _):
-        some = reqg[g]
-        spot = lax.broadcasted_iota(jnp.int32, (HALF, 4 * ranges), 1)
-        for i in range(members):
-            at = pl.ds(pl.multiple_of(g * rows + i * HALF, HALF), HALF)
-            oha[at, :] = jnp.where(spot == some[:HALF, i : i + 1], 1.0, 0.0).astype(BF)
-            ohb[at, :] = jnp.where(spot == some[HALF:, i : i + 1], 1.0, 0.0).astype(BF)
-        return 0
-
-    lax.fori_loop(0, groups, one_hot, 0)
-
-    own_w.wait()
-    for d in range(3):
-        wcopies[d].wait_recv()
-    for g in range(4):
-        block = wr[g].astype(F32)
-        zero = jnp.zeros((128 - outs, hh), F32)
-        wx[0, :, g * 128 : (g + 1) * 128] = jnp.concatenate([block, zero], axis=0).T.astype(BF)
-        wx[1, :, g * 128 : (g + 1) * 128] = jnp.concatenate([zero, block], axis=0).T.astype(BF)
-    bias3 = column_of(b3[...])
-
-    for k, col in ((0, 0), (1, 3)):
-        e2[k].wait_recv()
-        place(col, jnp.maximum(acc_edge[k] + e2r[k].astype(F32), 0.0))
-
-    for g in range(groups):
-        at = slice(g * rows, (g + 1) * rows)
-        picked = jnp.dot(oha[at, :], h2t[0], preferred_element_type=F32)
-        picked += jnp.dot(ohb[at, :], h2t[1], preferred_element_type=F32)
-        pbuf[g] = picked.astype(BF)
-
-        def ship(i, _):
-            block = pl.ds(pl.multiple_of(i * HALF, HALF), HALF)
-            pltpu.make_async_remote_copy(
-                src_ref=pbuf.at[g, block],
-                dst_ref=arr.at[g, block],
-                send_sem=a_send.at[g],
-                recv_sem=a_recv.at[g],
-                device_id=(shifted(g, i, 1), ch),
-                device_id_type=MESH,
-            ).start()
-            return 0
-
-        lax.fori_loop(1 if g == 0 else 0, members, ship, 0)
-        if g == 0:
-            arr[0, :HALF, :] = pbuf[0, :HALF, :]
-
     def whole(g):
         size = rows - HALF if g == 0 else rows
         return pltpu.make_async_remote_copy(
@@ -440,45 +448,55 @@
             device_id_type=MESH,
         )
 
-    total_a = jnp.zeros((cart, 128), F32)
-    total_b = jnp.zeros((cart, 128), F32)
+    half = cart // 2
+    piece = half // 2
+    sums = {}
     for g in range(groups):
         whole(g).wait_recv()
         at = slice(g * rows, (g + 1) * rows)
-        total_a += jnp.dot(sa[:, at], arr[g], preferred_element_type=F32)
-        total_b += jnp.dot(sb[:, at], arr[g], preferred_element_type=F32)
-
-    half = cart // 2
-    lane = lax.broadcasted_iota(jnp.int32, (half, 128), 1)
-    first = total_a[:half] + pltpu.roll(total_b[:half], 64, 1)
-    second = pltpu.roll(total_a[half:], 64, 1) + total_b[half:]
-    rbuf[ch] = jnp.where(lane < 64, first, second).astype(BF)
-    rcopies = []
-    for d in range(1, 4):
-        c = pltpu.make_async_remote_copy(
-            src_ref=rbuf.at[ch],
-            dst_ref=rbuf.at[ch],
-            send_sem=r_send.at[d - 1],
-            recv_sem=r_recv.at[d - 1],
-            device_id=(az, peers[d]),
-            device_id_type=MESH,
-        )
-        c.start()
-        rcopies.append(c)
-    for c in rcopies:
-        c.wait_recv()
-    for p in range(2):
-        sum_p = jnp.zeros((hh, half), F32)
-        for g in range(4):
-            sum_p += lax.dot_general(
-                wx[p, :, g * 128 : (g + 1) * 128],
-                rbuf[g],
-                (((1,), (1,)), ((), ())),
-                preferred_element_type=F32,
+        for h in range(2):
+            for p in range(2):
+                cells = slice(p * half + h * piece, p * half + (h + 1) * piece)
+                for name, ref in (("a", sa), ("b", sb)):
+                    term = jnp.dot(ref[cells, at], arr[g], preferred_element_type=F32)
+                    key = (h, p, name)
+                    sums[key] = term if g == 0 else sums[key] + term
+    lane = lax.broadcasted_iota(jnp.int32, (piece, 128), 1)
+    rcopies = {}
+    for h in range(2):
+        first = sums[h, 0, "a"] + pltpu.roll(sums[h, 0, "b"], 64, 1)
+        second = pltpu.roll(sums[h, 1, "a"], 64, 1) + sums[h, 1, "b"]
+        at = slice(h * piece, (h + 1) * piece)
+        rbuf[ch, at, :] = jnp.where(lane < 64, first, second).astype(BF)
+        rcopies[h] = []
+        for d in (3, 2, 1):
+            c = pltpu.make_async_remote_copy(
+                src_ref=rbuf.at[ch, at],
+                dst_ref=rbuf.at[ch, at],
+                send_sem=r_send.at[h, d - 1],
+                recv_sem=r_recv.at[h, d - 1],
+                device_id=(az, peers[d]),
+                device_id_type=MESH,
             )
-        out[:, p * half : (p + 1) * half] = (sum_p + bias3).astype(BF)
-
-    for c in e1 + e2 + wcopies + passed + rcopies + [c for k in range(4) for c in gathers[k]]:
+            c.start()
+            rcopies[h].append(c)
+    for h in range(2):
+        for c in rcopies[h]:
+            c.wait_recv()
+        at = slice(h * piece, (h + 1) * piece)
+        for p in range(2):
+            sum_p = jnp.zeros((hh, piece), F32)
+            for g in range(4):
+                sum_p += lax.dot_general(
+                    wx[p, :, g * 128 : (g + 1) * 128],
+                    rbuf[g, at, :],
+                    (((1,), (1,)), ((), ())),
+                    preferred_element_type=F32,
+                )
+            cells = slice(p * half + h * piece, p * half + (h + 1) * piece)
+            out[:, cells] = (sum_p + bias3).astype(BF)
+
+    for c in e1 + e2 + wcopies + passed + rcopies[0] + rcopies[1] + [c for k in range(4) for c in gathers[k]]:
         c.wait_send()
 
     @pl.when(ch == 0)
@@ -579,18 +597,18 @@
             dma((3,)),
             dma((4, 3)),
             dma((4, 3)),
-            dma((3,)),
-            dma((3,)),
+            dma((2, 3)),
+            dma((2, 3)),
             dma((groups,)),
             dma((groups,)),
         ],
         compiler_params=pltpu.CompilerParams(
-            collective_id=0, has_side_effects=True, vmem_limit_bytes=60 * 1024 * 1024
+            collective_id=0, has_side_effects=True, vmem_limit_bytes=48 * 1024 * 1024
         ),
         cost_estimate=pl.CostEstimate(
             flops=4 * 10**9, bytes_accessed=2 * 10**6, transcendentals=0
         ),
-    )(*args)
+    )(*[pltpu.with_memory_space_constraint(x, pltpu.HBM) for x in args])
 
 
 def solution(mesh):

time: 59.3 us -> 57.8 us (0.975)
  local copies, waits for them, and re-layouts: 1.57 us -> 0.66 us
  Pallas kernels: 57.6 us -> 57 us
    unnamed x1, local copies, waits for them, and re-layouts: 1.57 us -> 0.66 us
    pallas_call x1, Pallas kernels: 57.6 us -> 57 us  [local(): pl.pallas_call(functools.partial(kernel, n), out_shape=jax.ShapeDtypeStru...]
where the time goes in v4:
time: 57.8 us; the launch traced here: 57.7 us
  Pallas kernels  57 us (99%)
  local copies, waits for them, and re-layouts  0.66 us (1%)
    pallas_call x1, Pallas kernels, local(): pl.pallas_call(functools.partial(kernel, n), out_shape=jax.ShapeDtypeStru...  57 us

profile of v4, /device:TPU:1, one launch (start us, length us, event | category | flops | bytes accessed | tf_op | source)
XLA Modules:
  0.0 57.7 jit_solution(17913083344813217902)
XLA Ops:
  0.0 57.0 %shard_map.100 = bf16[128,512]{1,0:T(8,128)(2,1)S(1)} custom-call(bf16[256,4,256]{2,1,0:T(4,128)(2,1)} %feat.1, bf16[576,256]{1,0:T(8,128)(2,1)} %bitcast.10, f32[1,64]{1,0:T(1,128)} %bitcast.13, bf16[576,256]{1,0:T(8,128)(2,1)} %bitcast.11, f32[1,64]{1,0:T(1,128)} %bitcast.14, s32[32,1,128]{2,1,0:T(1,128)} %bitcast.12, s32[4,512]{1,0:T(4,128)} %slot_in.1, ...), custom_call_target="tpu_custom_call" | custom-call | flops 4000000000 | bytes 2000000 | tf_op jit(solution)/shard_map/pallas_call | solution.py:550
  57.1 0.7 %copy.12 = bf16[128,512]{1,0:T(8,128)(2,1)} copy(bf16[128,512]{1,0:T(8,128)(2,1)S(1)} %shard_map.100) | data formatting | bytes 262144

commit v5 on v4

--- a/solution.py
+++ b/solution.py
@@ -57,8 +57,6 @@
     h1,
     e1s,
     e1r,
-    e2s,
-    e2r,
     acc_edge,
     oha,
     ohb,
@@ -78,8 +76,6 @@
     in_sem,
     e1_send,
     e1_recv,
-    e2_send,
-    e2_recv,
     rq_send,
     rq_recv,
     rg_send,
@@ -155,25 +151,28 @@
     def at_column(col):
         return slice(col * chans, (col + 1) * chans)
 
-    def part(w, x, col):
+    def part(w, x, col, begin, end):
         total = None
         for tap in range(3):
             src = col + tap - 1
-            if 0 <= src <= 3:
+            if begin <= src <= end:
                 term = jnp.dot(
                     w[tap * 3 * outs : (tap + 1) * 3 * outs, :],
-                    x[at_column(src), :],
+                    x[at_column(src - begin), :],
                     preferred_element_type=F32,
                 )
                 total = term if total is None else total + term
         return combine(total, outs, ranges)
 
     fetches[0].wait()
-    for col in (3, 0):
+    for col in (3, 2, 0, 1):
         x1[at_column(col), :] = fv[:, col, :]
     fetches[1].wait()
-    e1s[0] = part(w1, x1, 4).astype(BF)
-    e1s[1] = part(w1, x1, -1).astype(BF)
+    edges = ((2, 3), (3, 4), (0, -1), (1, 0))
+    for k, col in edges:
+        mine_only = part(w1, x1, col, 0, 3)
+        acc_edge[k] = mine_only
+        e1s[1 - k // 2, (k % 2) * outs : (k % 2 + 1) * outs, :] = mine_only.astype(BF)
     fetches[2].wait()
 
     pl.semaphore_wait(barrier, n + 2)
@@ -253,23 +252,21 @@
     for k in range(1, share):
         ask(k)
 
-    for col in (1, 2):
-        x1[at_column(col), :] = fv[:, col, :]
     fetches[3].wait()
     bias1 = column_of(b1[...])
 
     def mine(col):
-        return pl.ds(pl.multiple_of(col * chans + ch * outs, outs), outs)
+        return pl.ds(pl.multiple_of((col + 1) * chans + ch * outs, outs), outs)
 
     def block_of(col, owner):
-        return pl.ds(pl.multiple_of(col * chans + owner * outs, outs), outs)
+        return pl.ds(pl.multiple_of((col + 1) * chans + owner * outs, outs), outs)
 
     def pass_block(col, owner, to, lane):
         c = pltpu.make_async_remote_copy(
             src_ref=h1.at[block_of(col, owner)],
             dst_ref=h1.at[block_of(col, owner)],
-            send_sem=g_send.at[col, lane - 1],
-            recv_sem=g_recv.at[col, lane - 1],
+            send_sem=g_send.at[col + 1, lane - 1],
+            recv_sem=g_recv.at[col + 1, lane - 1],
             device_id=(az, peers[to]),
             device_id_type=MESH,
         )
@@ -278,10 +275,8 @@
 
     gathers = {}
     for col in (1, 2):
-        h1[mine(col), :] = jnp.maximum(part(w1, x1, col) + bias1, 0.0).astype(BF)
+        h1[mine(col), :] = jnp.maximum(part(w1, x1, col, 0, 3) + bias1, 0.0).astype(BF)
         gathers[col] = [pass_block(col, ch, d, d) for d in (2, 1)]
-    for k, col in ((1, 3), (0, 0)):
-        acc_edge[k] = part(w1, x1, col) + bias1
 
     def asked(ref, at, count, send, recv):
         return pltpu.make_async_remote_copy(
@@ -293,26 +288,16 @@
             device_id_type=MESH,
         )
 
-    for k, col in ((1, 3), (0, 0)):
-        e1[k].wait_recv()
-        h1[mine(col), :] = jnp.maximum(acc_edge[k] + e1r[k].astype(F32), 0.0).astype(BF)
-        gathers[col] = [pass_block(col, ch, d, d) for d in (3, 2, 1)]
+    for c in e1:
+        c.wait_recv()
+    late = ((1, 0), (2, 3), (0, -1), (3, 4))
+    for k, col in late:
+        other = e1r[k // 2, (k % 2) * outs : (k % 2 + 1) * outs, :].astype(F32)
+        h1[mine(col), :] = jnp.maximum(acc_edge[k] + other + bias1, 0.0).astype(BF)
+        gathers[col] = [pass_block(col, ch, d, d) for d in (2, 1)]
     for col in (1, 2):
         gathers[col][0].wait_recv()
         gathers[col].append(pass_block(col, peers[2], 1, 3))
-
-    own_w.wait()
-    for d in range(3):
-        wcopies[d].wait_recv()
-    for g in range(4):
-        block = wr[g].astype(F32)
-        zero = jnp.zeros((128 - outs, hh), F32)
-        wx[0, :, g * 128 : (g + 1) * 128] = jnp.concatenate([block, zero], axis=0).T.astype(BF)
-        wx[1, :, g * 128 : (g + 1) * 128] = jnp.concatenate([zero, block], axis=0).T.astype(BF)
-    for k in (4, 5, 8):
-        fetches[k].wait()
-    bias2 = column_of(b2[...])
-    bias3 = column_of(b3[...])
 
     asked(rq, 0, share, rq_send, rq_recv).wait_recv()
     passed = []
@@ -329,16 +314,22 @@
         c.start()
         passed.append(c)
 
-    e2 = edge(e2s, e2r, e2_send, e2_recv)
-    for k, col, to in ((0, 3, 4), (1, 0, -1)):
-        for c in gathers[col]:
-            c.wait_recv()
-        e2s[k] = part(w2, h1, to).astype(BF)
-        e2[k].start()
-    gathers[1][1].wait_recv()
-    gathers[1][2].wait_recv()
-    gathers[2][1].wait_recv()
-    gathers[2][2].wait_recv()
+    own_w.wait()
+    for d in range(3):
+        wcopies[d].wait_recv()
+    for g in range(4):
+        block = wr[g].astype(F32)
+        zero = jnp.zeros((128 - outs, hh), F32)
+        wx[0, :, g * 128 : (g + 1) * 128] = jnp.concatenate([block, zero], axis=0).T.astype(BF)
+        wx[1, :, g * 128 : (g + 1) * 128] = jnp.concatenate([zero, block], axis=0).T.astype(BF)
+    for k in (4, 5, 8):
+        fetches[k].wait()
+    bias2 = column_of(b2[...])
+    bias3 = column_of(b3[...])
+
+    for k, col in late:
+        gathers[col][0].wait_recv()
+        gathers[col].append(pass_block(col, peers[2], 1, 3))
 
     def place(col, value):
         zero = jnp.zeros((128 - outs, ranges), F32)
@@ -346,10 +337,19 @@
         h2t[0, at, :] = jnp.concatenate([value, zero], axis=0).T.astype(BF)
         h2t[1, at, :] = jnp.concatenate([zero, value], axis=0).T.astype(BF)
 
-    for col in (1, 2):
-        place(col, jnp.maximum(part(w2, h1, col) + bias2, 0.0))
-    for k, col in ((0, 0), (1, 3)):
-        acc_edge[k] = part(w2, h1, col) + bias2
+    def second(col):
+        place(col, jnp.maximum(part(w2, h1, col, -1, 4) + bias2, 0.0))
+
+    def arrived(col):
+        gathers[col][1].wait_recv()
+        gathers[col][2].wait_recv()
+
+    arrived(1)
+    arrived(2)
+    arrived(0)
+    second(1)
+    arrived(3)
+    second(2)
 
     for c in passed:
         c.wait_recv()
@@ -369,9 +369,10 @@
 
     lax.fori_loop(0, groups, one_hot, 0)
 
-    for k, col in ((0, 0), (1, 3)):
-        e2[k].wait_recv()
-        place(col, jnp.maximum(acc_edge[k] + e2r[k].astype(F32), 0.0))
+    arrived(-1)
+    second(0)
+    arrived(4)
+    second(3)
 
     for g in range(groups):
         at = slice(g * rows, (g + 1) * rows)
@@ -496,7 +497,7 @@
             cells = slice(p * half + h * piece, p * half + (h + 1) * piece)
             out[:, cells] = (sum_p + bias3).astype(BF)
 
-    for c in e1 + e2 + wcopies + passed + rcopies[0] + rcopies[1] + [c for k in range(4) for c in gathers[k]]:
+    for c in e1 + wcopies + passed + rcopies[0] + rcopies[1] + [c for k in range(-1, 5) for c in gathers[k]]:
         c.wait_send()
 
     @pl.when(ch == 0)
@@ -563,12 +564,10 @@
             pltpu.VMEM((4, cart), jnp.int32),
             pltpu.VMEM((2, cart), F32),
             pltpu.VMEM((1, hh), F32),
-            pltpu.VMEM((4 * chans, ranges), BF),
-            pltpu.VMEM((2, outs, ranges), BF),
-            pltpu.VMEM((2, outs, ranges), BF),
-            pltpu.VMEM((2, outs, ranges), BF),
-            pltpu.VMEM((2, outs, ranges), BF),
-            pltpu.VMEM((2, outs, ranges), F32),
+            pltpu.VMEM((6 * chans, ranges), BF),
+            pltpu.VMEM((2, 2 * outs, ranges), BF),
+            pltpu.VMEM((2, 2 * outs, ranges), BF),
+            pltpu.VMEM((4, outs, ranges), F32),
             pltpu.VMEM((n * HALF, 4 * ranges), BF),
             pltpu.VMEM((n * HALF, 4 * ranges), BF),
             pltpu.VMEM((cart, n * HALF), BF),
@@ -587,16 +586,14 @@
             dma((10,)),
             dma((2,)),
             dma((2,)),
-            dma((2,)),
-            dma((2,)),
             dma,
             dma,
             dma((3,)),
             dma((3,)),
             dma((3,)),
             dma((3,)),
-            dma((4, 3)),
-            dma((4, 3)),
+            dma((6, 3)),
+            dma((6, 3)),
             dma((2, 3)),
             dma((2, 3)),
             dma((groups,)),

time: 57.8 us -> 59.9 us (1.036)
  Pallas kernels: 57 us -> 59.1 us
    pallas_call x1, Pallas kernels: 57 us -> 59.1 us  [local(): pl.pallas_call(functools.partial(kernel, n), out_shape=jax.ShapeDtypeStru...]
where the time goes in v5:
time: 59.9 us; the launch traced here: 59.8 us
  Pallas kernels  59.1 us (99%)
  local copies, waits for them, and re-layouts  0.66 us (1%)
    pallas_call x1, Pallas kernels, local(): pl.pallas_call(functools.partial(kernel, n), out_shape=jax.ShapeDtypeStru...  59.1 us

profile of v5, /device:TPU:1, one launch (start us, length us, event | category | flops | bytes accessed | tf_op | source)
XLA Modules:
  0.0 59.8 jit_solution(125276370275046998)
XLA Ops:
  0.0 59.1 %shard_map.100 = bf16[128,512]{1,0:T(8,128)(2,1)S(1)} custom-call(bf16[256,4,256]{2,1,0:T(4,128)(2,1)} %feat.1, bf16[576,256]{1,0:T(8,128)(2,1)} %bitcast.10, f32[1,64]{1,0:T(1,128)} %bitcast.13, bf16[576,256]{1,0:T(8,128)(2,1)} %bitcast.11, f32[1,64]{1,0:T(1,128)} %bitcast.14, s32[32,1,128]{2,1,0:T(1,128)} %bitcast.12, s32[4,512]{1,0:T(4,128)} %slot_in.1, ...), custom_call_target="tpu_custom_call" | custom-call | flops 4000000000 | bytes 2000000 | tf_op jit(solution)/shard_map/pallas_call | solution.py:551
  59.2 0.7 %copy.12 = bf16[128,512]{1,0:T(8,128)(2,1)} copy(bf16[128,512]{1,0:T(8,128)(2,1)S(1)} %shard_map.100) | data formatting | bytes 262144

commit v6 on v5

--- a/solution.py
+++ b/solution.py
@@ -78,8 +78,6 @@
     e1_recv,
     rq_send,
     rq_recv,
-    rg_send,
-    rg_recv,
     w_send,
     w_recv,
     g_send,
@@ -100,7 +98,6 @@
     cart = slot.shape[1]
     rows = members * HALF
     hh = out.shape[0]
-    share = n // 4
     right = lax.rem(az + 1, n)
     left = lax.rem(az + n - 1, n)
     my_z = az // members
@@ -204,24 +201,25 @@
         ahead_xy.append(lax.rem(my_x + ix, nx) * ny + lax.rem(my_y + iy, ny))
         back_xy.append(lax.rem(my_x + nx - ix, nx) * ny + lax.rem(my_y + ny - iy, ny))
 
-    def ask(k):
-        p = ch * share + k
-        g = p // members
-        i = lax.rem(p, members) if share % members else k % members
-        if share % members:
-            ix, iy = i // ny, lax.rem(i, ny)
-            xy = lax.rem(my_x + nx - ix, nx) * ny + lax.rem(my_y + ny - iy, ny)
-        else:
-            xy = back_xy[i]
-        to = lax.rem(my_z + nz - lax.rem(g + i, nz), nz) * members + xy
+    def ask(g, i):
+        to = lax.rem(my_z + nz - lax.rem(g + i, nz), nz) * members + back_xy[i]
         pltpu.make_async_remote_copy(
             src_ref=req.at[to // 4],
-            dst_ref=rq.at[p],
+            dst_ref=rq.at[g * members + i],
             send_sem=rq_send,
             recv_sem=rq_recv,
             device_id=(to, ch),
             device_id_type=MESH,
         ).start()
+
+    def ask_first(g, _):
+        ask(g, 0)
+        return 0
+
+    def ask_rest(g, _):
+        for i in range(1, members):
+            ask(g, i)
+        return 0
 
     wcopies = []
     for d in range(1, 4):
@@ -241,16 +239,9 @@
     )
     own_w.start()
 
-    @pl.when(ch == 0)
-    def _():
-        pltpu.make_async_copy(req.at[az // 4], rq.at[0], rq_recv).start()
-
-    @pl.when(ch != 0)
-    def _():
-        ask(0)
-
-    for k in range(1, share):
-        ask(k)
+    lax.fori_loop(1, groups, ask_first, 0)
+    lax.fori_loop(0, groups, ask_rest, 0)
+    rq[0] = req[az // 4]
 
     fetches[3].wait()
     bias1 = column_of(b1[...])
@@ -278,12 +269,12 @@
         h1[mine(col), :] = jnp.maximum(part(w1, x1, col, 0, 3) + bias1, 0.0).astype(BF)
         gathers[col] = [pass_block(col, ch, d, d) for d in (2, 1)]
 
-    def asked(ref, at, count, send, recv):
+    def asked():
         return pltpu.make_async_remote_copy(
-            src_ref=ref.at[pl.ds(at, count)],
-            dst_ref=ref.at[pl.ds(at, count)],
-            send_sem=send,
-            recv_sem=recv,
+            src_ref=rq.at[pl.ds(1, n - 1)],
+            dst_ref=rq.at[pl.ds(1, n - 1)],
+            send_sem=rq_send,
+            recv_sem=rq_recv,
             device_id=(right, ch),
             device_id_type=MESH,
         )
@@ -299,20 +290,29 @@
         gathers[col][0].wait_recv()
         gathers[col].append(pass_block(col, peers[2], 1, 3))
 
-    asked(rq, 0, share, rq_send, rq_recv).wait_recv()
-    passed = []
-    for d in range(1, 4):
-        at = pl.ds(pl.multiple_of(ch * share, share), share)
-        c = pltpu.make_async_remote_copy(
-            src_ref=rq.at[at],
-            dst_ref=rq.at[at],
-            send_sem=rg_send.at[d - 1],
-            recv_sem=rg_recv.at[d - 1],
-            device_id=(az, peers[d]),
-            device_id_type=MESH,
-        )
-        c.start()
-        passed.append(c)
+    def hand_on(col):
+        gathers[col][0].wait_recv()
+        gathers[col].append(pass_block(col, peers[2], 1, 3))
+
+    asked().wait_recv()
+    reqt[...] = rq[:, 0, :].T
+    wanted = reqt[pl.ds(pl.multiple_of(lax.rem(az, 4) * 2 * HALF, 2 * HALF), 2 * HALF), :]
+    for g in range(groups):
+        reqg[g] = wanted[:, g * members : (g + 1) * members]
+
+    def one_hot(g, _):
+        some = reqg[g]
+        spot = lax.broadcasted_iota(jnp.int32, (HALF, 4 * ranges), 1)
+        for i in range(members):
+            at = pl.ds(pl.multiple_of(g * rows + i * HALF, HALF), HALF)
+            oha[at, :] = jnp.where(spot == some[:HALF, i : i + 1], 1.0, 0.0).astype(BF)
+            ohb[at, :] = jnp.where(spot == some[HALF:, i : i + 1], 1.0, 0.0).astype(BF)
+        return 0
+
+    lax.fori_loop(0, groups, one_hot, 0)
+
+    hand_on(0)
+    hand_on(3)
 
     own_w.wait()
     for d in range(3):
@@ -327,9 +327,8 @@
     bias2 = column_of(b2[...])
     bias3 = column_of(b3[...])
 
-    for k, col in late:
-        gathers[col][0].wait_recv()
-        gathers[col].append(pass_block(col, peers[2], 1, 3))
+    hand_on(-1)
+    hand_on(4)
 
     def place(col, value):
         zero = jnp.zeros((128 - outs, ranges), F32)
@@ -350,24 +349,6 @@
     second(1)
     arrived(3)
     second(2)
-
-    for c in passed:
-        c.wait_recv()
-    reqt[...] = rq[:, 0, :].T
-    wanted = reqt[pl.ds(pl.multiple_of(lax.rem(az, 4) * 2 * HALF, 2 * HALF), 2 * HALF), :]
-    for g in range(groups):
-        reqg[g] = wanted[:, g * members : (g + 1) * members]
-
-    def one_hot(g, _):
-        some = reqg[g]
-        spot = lax.broadcasted_iota(jnp.int32, (HALF, 4 * ranges), 1)
-        for i in range(members):
-            at = pl.ds(pl.multiple_of(g * rows + i * HALF, HALF), HALF)
-            oha[at, :] = jnp.where(spot == some[:HALF, i : i + 1], 1.0, 0.0).astype(BF)
-            ohb[at, :] = jnp.where(spot == some[HALF:, i : i + 1], 1.0, 0.0).astype(BF)
-        return 0
-
-    lax.fori_loop(0, groups, one_hot, 0)
 
     arrived(-1)
     second(0)
@@ -497,17 +478,10 @@
             cells = slice(p * half + h * piece, p * half + (h + 1) * piece)
             out[:, cells] = (sum_p + bias3).astype(BF)
 
-    for c in e1 + wcopies + passed + rcopies[0] + rcopies[1] + [c for k in range(-1, 5) for c in gathers[k]]:
+    for c in e1 + wcopies + rcopies[0] + rcopies[1] + [c for k in range(-1, 5) for c in gathers[k]]:
         c.wait_send()
 
-    @pl.when(ch == 0)
-    def _():
-        asked(rq, 0, share - 1, rq_send, rq_recv).wait_send()
-
-    @pl.when(ch != 0)
-    def _():
-        asked(rq, 0, share, rq_send, rq_recv).wait_send()
-
+    asked().wait_send()
     for g in range(groups):
         whole(g).wait_send()
 
@@ -590,8 +564,6 @@
             dma,
             dma((3,)),
             dma((3,)),
-            dma((3,)),
-            dma((3,)),
             dma((6, 3)),
             dma((6, 3)),
             dma((2, 3)),

time: 59.9 us -> 59.4 us (level)
  no operation moved by 1% of the time
where the time goes in v6:
time: 59.4 us; the launch traced here: 59.3 us
  Pallas kernels  58.6 us (99%)
  local copies, waits for them, and re-layouts  0.66 us (1%)
    pallas_call x1, Pallas kernels, local(): pl.pallas_call(functools.partial(kernel, n), out_shape=jax.ShapeDtypeStru...  58.6 us

profile of v6, /device:TPU:1, one launch (start us, length us, event | category | flops | bytes accessed | tf_op | source)
XLA Modules:
  0.0 59.3 jit_solution(2516552315924003706)
XLA Ops:
  0.0 58.6 %shard_map.100 = bf16[128,512]{1,0:T(8,128)(2,1)S(1)} custom-call(bf16[256,4,256]{2,1,0:T(4,128)(2,1)} %feat.1, bf16[576,256]{1,0:T(8,128)(2,1)} %bitcast.10, f32[1,64]{1,0:T(1,128)} %bitcast.13, bf16[576,256]{1,0:T(8,128)(2,1)} %bitcast.11, f32[1,64]{1,0:T(1,128)} %bitcast.14, s32[32,1,128]{2,1,0:T(1,128)} %bitcast.12, s32[4,512]{1,0:T(4,128)} %slot_in.1, ...), custom_call_target="tpu_custom_call" | custom-call | flops 4000000000 | bytes 2000000 | tf_op jit(solution)/shard_map/pallas_call | solution.py:525
  58.6 0.7 %copy.12 = bf16[128,512]{1,0:T(8,128)(2,1)} copy(bf16[128,512]{1,0:T(8,128)(2,1)S(1)} %shard_map.100) | data formatting | bytes 262144

commit v7 on v4

--- a/solution.py
+++ b/solution.py
@@ -279,7 +279,7 @@
     gathers = {}
     for col in (1, 2):
         h1[mine(col), :] = jnp.maximum(part(w1, x1, col) + bias1, 0.0).astype(BF)
-        gathers[col] = [pass_block(col, ch, d, d) for d in (2, 1)]
+        gathers[col] = [pass_block(col, ch, d, d) for d in (3, 2, 1)]
     for k, col in ((1, 3), (0, 0)):
         acc_edge[k] = part(w1, x1, col) + bias1
 
@@ -297,10 +297,6 @@
         e1[k].wait_recv()
         h1[mine(col), :] = jnp.maximum(acc_edge[k] + e1r[k].astype(F32), 0.0).astype(BF)
         gathers[col] = [pass_block(col, ch, d, d) for d in (3, 2, 1)]
-    for col in (1, 2):
-        gathers[col][0].wait_recv()
-        gathers[col].append(pass_block(col, peers[2], 1, 3))
-
     own_w.wait()
     for d in range(3):
         wcopies[d].wait_recv()
@@ -335,10 +331,9 @@
             c.wait_recv()
         e2s[k] = part(w2, h1, to).astype(BF)
         e2[k].start()
-    gathers[1][1].wait_recv()
-    gathers[1][2].wait_recv()
-    gathers[2][1].wait_recv()
-    gathers[2][2].wait_recv()
+    for col in (1, 2):
+        for c in gathers[col]:
+            c.wait_recv()
 
     def place(col, value):
         zero = jnp.zeros((128 - outs, ranges), F32)

time: 57.8 us -> 57.4 us (level)
  no operation moved by 1% of the time
where the time goes in v7:
time: 57.4 us; the launch traced here: 57.3 us
  Pallas kernels  56.6 us (99%)
  local copies, waits for them, and re-layouts  0.66 us (1%)
    pallas_call x1, Pallas kernels, local(): pl.pallas_call(functools.partial(kernel, n), out_shape=jax.ShapeDtypeStru...  56.6 us

profile of v7, /device:TPU:1, one launch (start us, length us, event | category | flops | bytes accessed | tf_op | source)
XLA Modules:
  0.0 57.3 jit_solution(7620091316501112683)
XLA Ops:
  0.0 56.6 %shard_map.100 = bf16[128,512]{1,0:T(8,128)(2,1)S(1)} custom-call(bf16[256,4,256]{2,1,0:T(4,128)(2,1)} %feat.1, bf16[576,256]{1,0:T(8,128)(2,1)} %bitcast.10, f32[1,64]{1,0:T(1,128)} %bitcast.13, bf16[576,256]{1,0:T(8,128)(2,1)} %bitcast.11, f32[1,64]{1,0:T(1,128)} %bitcast.14, s32[32,1,128]{2,1,0:T(1,128)} %bitcast.12, s32[4,512]{1,0:T(4,128)} %slot_in.1, ...), custom_call_target="tpu_custom_call" | custom-call | flops 4000000000 | bytes 2000000 | tf_op jit(solution)/shard_map/pallas_call | solution.py:545
  56.7 0.7 %copy.12 = bf16[128,512]{1,0:T(8,128)(2,1)} copy(bf16[128,512]{1,0:T(8,128)(2,1)S(1)} %shard_map.100) | data formatting | bytes 262144
